TPU v7x, 128 devices: a whole 4x4x4 slice. The times are simulated.
128 devices in a mesh: wide: 32 (over x, y, core), narrow: 4 (over z).
Axes of the slice: x: 4, y: 4, z: 4, core: 2. Of those that a mesh axis runs over, the one named last changes fastest.
Arguments:
- cache: bfloat16 [32, 8192, 128], P('wide', 'narrow'), may hold values from -6 to 6
- lookup_slots: int32 [32, 16384, 16], P('wide'), may hold values from 0 to 8191
- bag_lengths: int32 [32, 16384], P('wide'), may hold values from 1 to 16
- miss_rows: bfloat16 [32, 4096, 128], P('wide', 'narrow'), may hold values from -6 to 6
- miss_slots: int32 [32, 4096], P('wide', 'narrow'), may hold values from 0 to 8191, as said below
- holder_counts: int32 [32, 16], P('wide', 'narrow'), may hold values from 0 to 512, as said below
- w_first: bfloat16 [4096, 4096], P(None, 'narrow'), may hold values from -0.09375 to 0.09375
- b_first: float32 [4096], P('narrow'), may hold values from -4 to 4
- w_second: bfloat16 [4096, 4096], P('narrow'), may hold values from -0.09375 to 0.09375
- b_second: float32 [4096], P('narrow'), may hold values from -4 to 4
- w_out: bfloat16 [4096], P('narrow'), may hold values from -0.09375 to 0.09375
Outputs:
- top_hidden: bfloat16 [16384, 4096], P('wide', 'narrow')
- logits: float32 [16384], P('wide')
- cache_next: bfloat16 [32, 8192, 128], P('wide', 'narrow')
Inputs may be any that keep to these rules, and one draw needn't show every extreme that they name: `holder_counts`: entry h * 4 + o is the number of row blocks that holder h sections for owner o, the device holding slots o * 2048 to (o + 1) * 2048 - 1; a holder's counts sum to at most 1024, and this is reached by some holder of every table; the largest count, 512, is reached in every table. `miss_slots`: A holder's live entries are packed by owner, owner 0 first, as its counts say; each live entry names a slot of its owner, no slot twice in a table; entries past a holder's live ones are 0 and unused.
All inputs are finite; a program needn't handle non-finite values.
Results may differ from a plain program's by a relative error of at most 0.0076.
Values may be sent and summed in bfloat16 or wider, within the bound.
A program may use at most 128 MiB of HBM per device.

v0:
```python
import math

import jax
import jax.numpy as jnp
from jax import lax
from jax.sharding import PartitionSpec as P

SEND_CAP = 512


def laid_out(tiles, dim):
    tiles = jnp.moveaxis(tiles, 0, dim)
    lengths = tiles.shape
    return tiles.reshape(*lengths[:dim], lengths[dim] * lengths[dim + 1], *lengths[dim + 2 :])


def copy_for_each(x, axis):
    length = lax.axis_size(axis)
    return lax.all_to_all(jnp.broadcast_to(x[None], (length, *x.shape)), axis, 0, 0, tiled=True)


def gathered_copies(x, axis, dim):
    return laid_out(copy_for_each(x, axis), dim)


def of_everyone(x, axis):
    everything = copy_for_each(x, axis)
    return jnp.sum(everything, axis=0)


def pool_rows(cache_table, lookups, lengths, owner_index):
    slot_count = cache_table.shape[0]
    emb_width = cache_table.shape[1]
    batch_rows, bag_size = lookups.shape
    local_slots = lookups - owner_index * slot_count
    usable = jnp.arange(bag_size, dtype=jnp.int32)[None, :] < lengths[:, None]
    usable = usable & (local_slots >= 0) & (local_slots < slot_count)
    safe_slots = jnp.clip(local_slots, 0, slot_count - 1)
    block_rows = math.gcd(batch_rows, 2048)
    block_count = batch_rows // block_rows

    def pool_block(member):
        positions, keep = member
        gathered = jnp.take(cache_table, positions, axis=0).astype(jnp.float32)
        return jnp.sum(jnp.where(keep[..., None], gathered, jnp.zeros((), jnp.float32)), axis=1)

    pooled = lax.map(
        pool_block,
        (
            safe_slots.reshape(block_count, block_rows, bag_size),
            usable.reshape(block_count, block_rows, bag_size),
        ),
    )
    return pooled.reshape(batch_rows, emb_width)


def body(
    cache,
    lookup_slots,
    bag_lengths,
    miss_rows,
    miss_slots,
    holder_counts,
    w_first,
    b_first,
    w_second,
    b_second,
    w_out,
):
    wide_count = lax.axis_size("wide")
    narrow_count = lax.axis_size("narrow")
    owner_index = lax.axis_index("narrow")
    cache_table = cache[0]
    slot_count = cache_table.shape[0]
    emb_width = cache_table.shape[1]
    lookups = lookup_slots[0]
    lengths = bag_lengths[0]
    batch_rows, bag_size = lookups.shape
    owner_rows = batch_rows // wide_count
    quarter_rows = owner_rows // narrow_count
    whole_table = gathered_copies(cache_table, "narrow", 0)
    own_lookups = lax.dynamic_index_in_dim(
        lookups.reshape(wide_count, narrow_count, quarter_rows, bag_size),
        owner_index,
        1,
        keepdims=False,
    )
    own_lengths = lax.dynamic_index_in_dim(
        lengths.reshape(wide_count, narrow_count, quarter_rows), owner_index, 1, keepdims=False
    )
    own_pooled = pool_rows(
        whole_table,
        own_lookups.reshape(wide_count * quarter_rows, bag_size),
        own_lengths.reshape(wide_count * quarter_rows),
        0,
    )
    summed = own_pooled.reshape(1, wide_count, quarter_rows, emb_width).astype(jnp.bfloat16)
    arrived = lax.all_to_all(summed, "wide", split_axis=1, concat_axis=0, tiled=True)
    arrived = arrived.reshape(wide_count, quarter_rows, emb_width)
    pooled = lax.all_gather(arrived, "narrow", axis=1, tiled=True)
    first_slab = w_first.reshape(wide_count, emb_width, w_first.shape[1])
    first_terms = jnp.einsum("fbe,feh->bh", pooled, first_slab, preferred_element_type=jnp.float32)
    first_hidden = jnp.maximum(first_terms + b_first, 0.0).astype(jnp.bfloat16)
    second_terms = jnp.dot(first_hidden, w_second, preferred_element_type=jnp.float32)
    second_summed = lax.psum_scatter(second_terms, "narrow", scatter_dimension=1, tiled=True)
    top_hidden = jnp.maximum(second_summed + b_second, 0.0).astype(jnp.bfloat16)
    logit_terms = jnp.dot(top_hidden, w_out, preferred_element_type=jnp.float32)
    logits = of_everyone(logit_terms, "narrow")
    sectioned = miss_rows[0]
    sectioned_slots = miss_slots[0]
    sectioned_counts = holder_counts[0]
    hold_rows = sectioned.shape[0]
    send_cap = SEND_CAP
    starts = jnp.cumsum(sectioned_counts) - sectioned_counts
    column_ids = jnp.arange(send_cap, dtype=jnp.int32)
    live = column_ids[None, :] < sectioned_counts[:, None]
    sources = jnp.where(live, starts[:, None] + column_ids[None, :], -1).reshape(
        narrow_count * send_cap
    )
    selector = (sources[:, None] == jnp.arange(hold_rows, dtype=jnp.int32)[None, :]).astype(
        jnp.bfloat16
    )
    slab_rows = jnp.dot(selector, sectioned, preferred_element_type=jnp.float32).astype(
        jnp.bfloat16
    )
    slab_rows = slab_rows.reshape(narrow_count, send_cap, emb_width)
    slab_slots = jnp.where(
        sources >= 0, jnp.take(sectioned_slots, jnp.maximum(sources, 0), axis=0), -1
    )
    slab_slots = slab_slots.reshape(narrow_count, send_cap)
    got_rows, got_slots = (
        lax.all_to_all(slab_rows, "narrow", split_axis=0, concat_axis=0, tiled=True),
        lax.all_to_all(slab_slots, "narrow", split_axis=0, concat_axis=0, tiled=True),
    )
    arrived_rows = got_rows.reshape(narrow_count * send_cap, emb_width)
    arrived_slots = got_slots.reshape(narrow_count * send_cap)
    targets = arrived_slots - owner_index * slot_count
    kept = (arrived_slots >= 0) & (targets >= 0) & (targets < slot_count)
    targets = jnp.where(kept, targets, -1)
    placing = (targets[:, None] == jnp.arange(slot_count, dtype=jnp.int32)[None, :]).astype(
        jnp.bfloat16
    )
    placed = jnp.einsum("as,ae->se", placing, arrived_rows, preferred_element_type=jnp.float32)
    struck = jnp.sum(placing.astype(jnp.float32), axis=0) > 0.5
    cache_next = jnp.where(struck[:, None], placed.astype(jnp.bfloat16), cache_table)[None]
    return (top_hidden, logits, cache_next)


def solution(mesh):
    return jax.shard_map(
        body,
        mesh=mesh,
        in_specs=(
            P("wide", "narrow", None),
            P("wide", None, None),
            P("wide", None),
            P("wide", "narrow", None),
            P("wide", "narrow"),
            P("wide", "narrow"),
            P(None, "narrow"),
            P("narrow"),
            P("narrow", None),
            P("narrow"),
            P("narrow"),
        ),
        out_specs=(P("wide", "narrow"), P("wide"), P("wide", "narrow", None)),
        check_vma=False,
    )
```

profile of v0, /device:TPU:0, one launch (start us, length us, event | category | flops | bytes accessed | tf_op | source)
XLA Modules:
  0.0 502.1 jit_solution(12865741644556562473)
XLA Ops:
  7.2 2.7 broadcast_in_dim.85
  9.9 5.4 %all-to-all-start = ((bf16[4,2048,128]{2,1,0:T(8,128)(2,1)}), bf16[4,2048,128]{2,1,0:T(8,128)(2,1)S(1)}, u32[]{:S(2)}, u32[]{:S(2)}) async-start(bf16[4,2048,128]{2,1,0:T(8,128)(2,1)} %broadcast_in_dim.85), calls=%async_computation | async-start | bytes 4194304 | tf_op jit(solution)/shard_map/all_to_all | solution.py:19
  15.3 1.9 reshape_squeeze.7
  18.2 2.6 copy.24
  21.7 3.5 broadcast_clamp_fusion.1
  25.9 1.9 fusion.14
  27.8 13.8 %all-to-all-done = bf16[4,2048,128]{2,1,0:T(8,128)(2,1)S(1)} async-done(((bf16[4,2048,128]{2,1,0:T(8,128)(2,1)}), bf16[4,2048,128]{2,1,0:T(8,128)(2,1)S(1)}, u32[]{:S(2)}, u32[]{:S(2)}) %all-to-all-start) | async-done | bytes 2097184 | tf_op jit(solution)/shard_map/all_to_all | solution.py:19
  41.6 266.1 %while.10 = (s32[]{:T(128)}, bf16[2,2048,128]{2,1,0:T(8,128)(2,1)}, pred[2,2048,16]{2,1,0:T(8,128)(4,1)}, s32[2,2048,16]{2,1,0:T(8,128)}, bf16[8192,128]{1,0:T(8,128)(2,1)S(1)}, /*index=5*/s32[]{:T(128)}) while((s32[]{:T(128)}, bf16[2,2048,128]{2,1,0:T(8,128)(2,1)}, pred[2,2048,16]{2,1,0:T(8,128)(4,1)}, s32[2,2048,16]{2,1,0:T(8,128)}, ...), condition=%wide.region_2.3_spmd, body=%wide.region_0.2_spmd.sunk | while | flops 16842752 | bytes 36602024 | solution.py:47
  43.3 114.9 %gather_fusion = bf16[32768,128]{1,0:T(8,128)(2,1)} fusion(bf16[8192,128]{1,0:T(8,128)(2,1)S(1)} %get-tuple-element.92, s32[32768]{0:T(1024)S(1)} %broadcast_clamp_fusion.4), kind=kCustom, calls=%fused_computation.clone.1 | custom fusion | bytes 16908288 | tf_op jit(solution)/shard_map/while/body/eval_jaxpr/jit(_take)/gather | solution.py:44
  159.8 13.8 %select_reduce_fusion.2 = bf16[2048,128]{1,0:T(8,128)(2,1)S(1)} fusion(pred[2048,16]{1,0:T(8,128)(4,1)S(1)} %compare_and_fusion.2, pred[2048,16]{1,0:T(8,128)(4,1)S(1)} %dynamic-slice_bitcast_fusion.2, bf16[32768,128]{1,0:T(8,128)(2,1)} %gather_fusion), kind=kLoop, calls=%fused_computation.2.clone.1 | loop fusion | flops 16515072 | bytes 8978432 | tf_op jit(solution)/shard_map/while/body/eval_jaxpr/reduce_sum | solution.py:45
  176.3 114.9 %gather_fusion = bf16[32768,128]{1,0:T(8,128)(2,1)} fusion(bf16[8192,128]{1,0:T(8,128)(2,1)S(1)} %get-tuple-element.92, s32[32768]{0:T(1024)S(1)} %broadcast_clamp_fusion.4), kind=kCustom, calls=%fused_computation.clone.1 | custom fusion | bytes 16908288 | tf_op jit(solution)/shard_map/while/body/eval_jaxpr/jit(_take)/gather | solution.py:44
  292.8 13.8 %select_reduce_fusion.2 = bf16[2048,128]{1,0:T(8,128)(2,1)S(1)} fusion(pred[2048,16]{1,0:T(8,128)(4,1)S(1)} %compare_and_fusion.2, pred[2048,16]{1,0:T(8,128)(4,1)S(1)} %dynamic-slice_bitcast_fusion.2, bf16[32768,128]{1,0:T(8,128)(2,1)} %gather_fusion), kind=kLoop, calls=%fused_computation.2.clone.1 | loop fusion | flops 16515072 | bytes 8978432 | tf_op jit(solution)/shard_map/while/body/eval_jaxpr/reduce_sum | solution.py:45
  307.7 24.2 %all_to_all.31 = bf16[1,32,128,128]{3,2,0,1:T(8,128)(2,1)} all-to-all(bf16[1,32,128,128]{3,2,0,1:T(8,128)(2,1)} %bitcast.95), channel_id=1, replica_groups=mesh['wide'=32,'narrow'=4] {'wide'}, dimensions={1} | all-to-all | bytes 2097152 | tf_op jit(solution)/shard_map/all_to_all | solution.py:98
  332.0 44.8 %all-gather.3.cloned.1.call-done = bf16[1,32,512,128]{3,2,1,0:T(8,128)(2,1)} async-done(((bf16[1,32,128,128]{3,2,1,0:T(8,128)(2,1)}), bf16[1,32,512,128]{3,2,1,0:T(8,128)(2,1)}) %all-gather.3.cloned.1.call-update) | async-done | bytes 4194320 | tf_op jit(solution)/shard_map/all_gather | solution.py:100
  376.8 19.0 %fusion.19 = f32[512,4096]{1,0:T(8,128)} fusion(bf16[1024,4096]{1,0:T(8,128)(2,1)} %param.21, bf16[32,128,1024]{2,1,0:T(8,128)(2,1)} %bitcast.109, bf16[1,32,512,128]{3,2,1,0:T(8,128)(2,1)} %all-gather.3.cloned.1.call-done, f32[1024]{0:T(1024)S(1)} %copy-done.11), kind=kOutput, calls=%fused_computation.49 | convolution fusion | flops 8591507456 | bytes 29364224 | tf_op jit(solution)/shard_map/dot_general | solution.py:104
  396.7 8.6 %gather_fusion.1 = s32[2048]{0:T(1024)S(1)} fusion(s32[1024]{0:T(1024)S(1)} %bitcast.90, s32[2048]{0:T(1024)S(1)} %broadcast_clamp_fusion.2), kind=kCustom, calls=%fused_computation.1 | custom fusion | bytes 24576 | tf_op jit(solution)/shard_map/jit(_take)/gather | solution.py:128
  406.0 3.4 all-to-all-start.3
  409.5 2.4 fusion.7
  411.9 2.9 all-to-all-done.3
  414.8 3.5 all-to-all-start.4
  418.4 2.1 convert_reduce_fusion
  420.4 62.2 %reduce-scatter.2.cloned.1.call-done = f32[512,1024]{1,0:T(8,128)} async-done(((f32[512,4096]{1,0:T(8,128)}), f32[512,1024]{1,0:T(8,128)}) %reduce-scatter.2.cloned.1.call-update) | async-done | bytes 2097168 | tf_op jit(solution)/shard_map/reduce_scatter | solution.py:105
  485.5 3.2 all-to-all-start.2
  488.8 5.8 %fusion.10 = bf16[1,2048,128]{2,1,0:T(8,128)(2,1)} fusion(bf16[2048,128]{1,0:T(8,128)(2,1)S(1)} %bitcast.97, s32[2048]{0:T(1024)S(1)} %and_select_fusion, pred[2048]{0:T(1024)(128)(4,1)S(1)} %broadcast_compare_fusion.2, bf16[1,2048,128]{2,1,0:T(8,128)(2,1)S(1)} %copy-done.7), kind=kOutput, calls=%fused_computation.22 | convolution fusion | flops 1078460416 | bytes 1583104 | tf_op jit(solution)/shard_map/as,ae->se/dot_general | solution.py:143
  (70 shorter events, 16.3 us)
Async XLA Ops:
  7.2 402.3 %copy-start = (bf16[1,1024,128]{2,1,0:T(8,128)(2,1)S(1)}, bf16[1,1024,128]{2,1,0:T(8,128)(2,1)}, u32[]{:S(2)}) copy-start(bf16[1,1024,128]{2,1,0:T(8,128)(2,1)} %param.16) | copy-start | bytes 786436
  9.9 31.7 %all-to-all-start = ((bf16[4,2048,128]{2,1,0:T(8,128)(2,1)}), bf16[4,2048,128]{2,1,0:T(8,128)(2,1)S(1)}, u32[]{:S(2)}, u32[]{:S(2)}) async-start(bf16[4,2048,128]{2,1,0:T(8,128)(2,1)} %broadcast_in_dim.85), calls=%async_computation | async-start | bytes 4194304 | tf_op jit(solution)/shard_map/all_to_all | solution.py:19
  15.3 361.5 %all-gather.3.cloned.1.call-start = ((), (), s32[]{:S(2)}) async-start(), calls=%async_computation.7 | async-start | bytes 5242880 | tf_op jit(solution)/shard_map/all_gather | solution.py:100
  21.7 3.5 copy-start.2
  41.6 335.2 %copy-start.11 = (f32[1024]{0:T(1024)S(1)}, f32[1024]{0:T(1024)}, u32[]{:S(2)}) copy-start(f32[1024]{0:T(1024)} %param.20) | copy-start | bytes 12292
  43.3 116.5 %copy-start.3 = (pred[2,2048,16]{2,1,0:T(8,128)(4,1)S(1)}, pred[2,2048,16]{2,1,0:T(8,128)(4,1)}, u32[]{:S(2)}) copy-start(pred[2,2048,16]{2,1,0:T(8,128)(4,1)} %get-tuple-element.90) | copy-start | bytes 196612 | tf_op jit(solution)/shard_map/while
  159.8 13.8 %copy-start.5 = (bf16[2,2048,128]{2,1,0:T(8,128)(2,1)S(1)}, bf16[2,2048,128]{2,1,0:T(8,128)(2,1)}, u32[]{:S(2)}) copy-start(bf16[2,2048,128]{2,1,0:T(8,128)(2,1)} %get-tuple-element.83) | copy-start | bytes 3145732 | tf_op jit(solution)/shard_map/while
  173.7 1.0 copy-start.6
  176.3 116.5 %copy-start.3 = (pred[2,2048,16]{2,1,0:T(8,128)(4,1)S(1)}, pred[2,2048,16]{2,1,0:T(8,128)(4,1)}, u32[]{:S(2)}) copy-start(pred[2,2048,16]{2,1,0:T(8,128)(4,1)} %get-tuple-element.90) | copy-start | bytes 196612 | tf_op jit(solution)/shard_map/while
  292.8 13.8 %copy-start.5 = (bf16[2,2048,128]{2,1,0:T(8,128)(2,1)S(1)}, bf16[2,2048,128]{2,1,0:T(8,128)(2,1)}, u32[]{:S(2)}) copy-start(bf16[2,2048,128]{2,1,0:T(8,128)(2,1)} %get-tuple-element.83) | copy-start | bytes 3145732 | tf_op jit(solution)/shard_map/while
  306.7 1.0 copy-start.6
  331.9 150.7 %reduce-scatter.2.cloned.1.call-start = ((), (), s32[]{:S(2)}) async-start(), calls=%async_computation.6 | async-start | bytes 10485760 | tf_op jit(solution)/shard_map/reduce_scatter | solution.py:105
  395.8 0.7 copy-start.10
  395.8 0.9 copy-start.1
  405.3 6.6 %copy-start.9 = (bf16[1024]{0:T(1024)(128)(2,1)S(1)}, bf16[1024]{0:T(1024)(128)(2,1)}, u32[]{:S(2)}) copy-start(bf16[1024]{0:T(1024)(128)(2,1)} %param.23) | copy-start | bytes 6148
  405.3 77.3 %copy-start.8 = (f32[1024]{0:T(1024)S(1)}, f32[1024]{0:T(1024)}, u32[]{:S(2)}) copy-start(f32[1024]{0:T(1024)} %param.22) | copy-start | bytes 12292
  406.0 8.8 %all-to-all-start.3 = ((s32[4,1,512]{2,1,0:T(1,128)}), s32[4,1,512]{2,1,0:T(1,128)S(1)}, u32[]{:S(2)}, u32[]{:S(2)}) async-start(s32[4,1,512]{2,1,0:T(1,128)} %compare_select_fusion.3), calls=%async_computation.4 | async-start | bytes 16384 | tf_op jit(solution)/shard_map/all_to_all | solution.py:133
  409.5 79.3 %copy-start.7 = (bf16[1,2048,128]{2,1,0:T(8,128)(2,1)S(1)}, bf16[1,2048,128]{2,1,0:T(8,128)(2,1)}, u32[]{:S(2)}) copy-start(bf16[1,2048,128]{2,1,0:T(8,128)(2,1)} %param.13) | copy-start | bytes 1572868
  414.8 70.1 %all-to-all-start.4 = ((bf16[4,512,128]{2,1,0:T(8,128)(2,1)}), bf16[4,512,128]{2,1,0:T(8,128)(2,1)S(1)}, u32[]{:S(2)}, u32[]{:S(2)}) async-start(bf16[4,512,128]{2,1,0:T(8,128)(2,1)} %bitcast.24), calls=%async_computation.5 | async-start | bytes 1048576 | tf_op jit(solution)/shard_map/all_to_all | solution.py:132
  484.5 10.1 %copy-start.4 = (bf16[512,1024]{1,0:T(8,128)(2,1)}, bf16[512,1024]{1,0:T(8,128)(2,1)S(1)}, u32[]{:S(2)}) copy-start(bf16[512,1024]{1,0:T(8,128)(2,1)S(1)} %maximum_convert_fusion) | copy-start | bytes 3145732
  485.5 9.1 %all-to-all-start.2 = ((f32[4,1,512]{2,1,0:T(1,128)}), f32[4,1,512]{2,1,0:T(1,128)S(1)}, u32[]{:S(2)}, u32[]{:S(2)}) async-start(f32[4,1,512]{2,1,0:T(1,128)} %broadcast_in_dim.86), calls=%async_computation.3 | async-start | bytes 16384 | tf_op jit(solution)/shard_map/all_to_all | solution.py:19
Sparse Core Ops, SparseCore 0:
  332.0 44.6 all-gather.2
  395.9 86.6 reduce-scatter.1
where the time goes:
time: 504 us; the launch traced here: 502 us
  local copies, waits for them, and re-layouts  252 us (50%)
  waiting for transfers between devices  124 us (25%)
  other arithmetic  45 us (9%)
  matrix products  27.6 us (5%)
  blocking collectives  24.2 us (5%)
  starting transfers between devices  15.6 us (3%)
  between operations  14.2 us (3%)
    gather x2, local copies, waits for them, and re-layouts, pool_block(): gathered = jnp.take(cache_table, positions, axis=0).astype(jnp.float32)  230 us
    reduce_scatter x1, waiting for transfers between devices, body(): lax.psum_scatter(second_terms, 'narrow', scatter_dimension=1, tiled=True)  62.2 us
    all_gather x1, waiting for transfers between devices, body(): pooled = lax.all_gather(arrived, 'narrow', axis=1, tiled=True)  44.8 us
    reduce_sum x2, other arithmetic, pool_block(): jnp.sum(jnp.where(keep[..., None], gathered, jnp.zeros((), jnp.float32)),...  27.5 us
    all_to_all x1, blocking collectives, body(): lax.all_to_all(summed, 'wide', split_axis=1, concat_axis=0, tiled=True)  24.2 us
    dot_general x1, matrix products, body(): jnp.dot(first_hidden, w_second, preferred_element_type=jnp.float32)  19 us
    all_to_all x2, waiting for transfers between devices, copy_for_each(): lax.all_to_all(jnp.broadcast_to(x[None], (length, *x.shape)), axis, 0, 0,...  13.8 us
  transfers between devices with their start and end apart: 6, of which 4 were waited for; matrix products, arithmetic and copies ran while one was open for 7% of the time, Pallas kernels for 0%

commit v1 on v0

v1 whole, which is shorter than its diff:
```python
import functools

import jax
import jax.numpy as jnp
from jax import lax
from jax.experimental import pallas as pl
from jax.experimental.pallas import tpu as pltpu
from jax.sharding import PartitionSpec as P

CHUNKS = 1
PAD = 16
UNROLL = 16
OWNERS_A_STEP = 4


def copy_for_each(x, axis):
    length = lax.axis_size(axis)
    return lax.all_to_all(jnp.broadcast_to(x[None], (length, *x.shape)), axis, 0, 0, tiled=True)


def pool_kernel(bag_size, rows, first, count, owners, index_ref, table_ref, out_ref, wide_ref, sum_ref):
    slots = table_ref.shape[0]

    @pl.when(pl.program_id(0) == 0)
    def _():
        wide_ref[:slots, :] = table_ref[...].astype(jnp.float32)
        wide_ref[slots:, :] = jnp.zeros((PAD, table_ref.shape[1]), jnp.float32)

    per_owner = count // UNROLL

    def step(i, _):
        owner = i // per_owner
        row = (i % per_owner) * UNROLL
        base = owner * (bag_size * rows) + first + row
        for u in range(UNROLL):
            terms = [
                wide_ref[pl.ds(index_ref[base + (l * rows + u)], 1), :] for l in range(bag_size)
            ]
            while len(terms) > 1:
                terms = [terms[k] + terms[k + 1] for k in range(0, len(terms), 2)]
            sum_ref[pl.ds(owner * count + row + u, 1), :] = terms[0]
        return 0

    lax.fori_loop(0, owners * per_owner, step, 0)
    out_ref[...] = sum_ref[...].astype(out_ref.dtype)


def pool_rows(table, indices, bag_size, rows, first, count):
    owner_count = indices.shape[0] // (bag_size * rows)
    owners = OWNERS_A_STEP
    slots, width = table.shape
    return pl.pallas_call(
        functools.partial(pool_kernel, bag_size, rows, first, count, owners),
        out_shape=jax.ShapeDtypeStruct((owner_count * count, width), jnp.bfloat16),
        grid=(owner_count // owners,),
        in_specs=[
            pl.BlockSpec((owners * bag_size * rows,), lambda i: (i,), memory_space=pltpu.SMEM),
            pl.BlockSpec((slots, width), lambda i: (0, 0), pipeline_mode=pl.Buffered(1)),
        ],
        out_specs=pl.BlockSpec((owners * count, width), lambda i: (i, 0)),
        scratch_shapes=[
            pltpu.VMEM((slots + PAD, width), jnp.float32),
            pltpu.VMEM((owners * count, width), jnp.float32),
        ],
        compiler_params=pltpu.CompilerParams(vmem_limit_bytes=16 << 20),
        cost_estimate=pl.CostEstimate(
            flops=2 * owner_count * count * bag_size * width * 400,
            bytes_accessed=slots * width * 2,
            transcendentals=0,
        ),
        name="pool",
    )(indices, table)


def body(
    cache,
    lookup_slots,
    bag_lengths,
    miss_rows,
    miss_slots,
    holder_counts,
    w_first,
    b_first,
    w_second,
    b_second,
    w_out,
):
    wide_count = lax.axis_size("wide")
    narrow_count = lax.axis_size("narrow")
    position = lax.axis_index("narrow")
    cache_table = cache[0]
    slot_count, width = cache_table.shape
    batch_rows, bag_size = lookup_slots.shape[1:]
    owner_rows = batch_rows // wide_count
    rows = owner_rows // narrow_count

    whole_table = copy_for_each(cache_table, "narrow").reshape(narrow_count * slot_count, width)

    by_lookup = lookup_slots[0].T.reshape(bag_size, wide_count, narrow_count, rows)
    by_lookup = lax.dynamic_index_in_dim(by_lookup, position, 2, keepdims=False)
    lengths = bag_lengths[0].reshape(wide_count, narrow_count, rows)
    lengths = lax.dynamic_index_in_dim(lengths, position, 1, keepdims=False)
    used = jnp.arange(bag_size, dtype=jnp.int32)[:, None, None] < lengths[None]
    indices = jnp.where(used, by_lookup, narrow_count * slot_count)
    indices = indices.transpose(1, 0, 2).reshape(wide_count * bag_size * rows)

    count = rows // CHUNKS
    first_slab = w_first.reshape(wide_count, width, w_first.shape[1])
    tops, logit_terms = [], []
    for chunk in range(CHUNKS):
        pooled = pool_rows(whole_table, indices, bag_size, rows, chunk * count, count)
        pooled = pooled.reshape(wide_count, count, width)
        arrived = lax.all_to_all(pooled, "wide", split_axis=0, concat_axis=0, tiled=True)
        features = lax.all_gather(arrived, "narrow", axis=1, tiled=True)
        first_terms = jnp.einsum(
            "fbe,feh->bh", features, first_slab, preferred_element_type=jnp.float32
        )
        first_hidden = jnp.maximum(first_terms + b_first, 0.0).astype(jnp.bfloat16)
        second_terms = jnp.dot(first_hidden, w_second, preferred_element_type=jnp.float32)
        second_summed = lax.psum_scatter(
            second_terms.astype(jnp.bfloat16), "narrow", scatter_dimension=1, tiled=True
        ).astype(jnp.float32)
        top = jnp.maximum(second_summed + b_second, 0.0).astype(jnp.bfloat16)
        logit_terms.append(jnp.dot(top, w_out, preferred_element_type=jnp.float32).reshape(narrow_count, count))
        tops.append(top.reshape(narrow_count, count, top.shape[1]))
    top_hidden = jnp.stack(tops, axis=1).reshape(owner_rows, tops[0].shape[2])
    logit_term = jnp.stack(logit_terms, axis=1).reshape(owner_rows)
    logits = jnp.sum(copy_for_each(logit_term, "narrow"), axis=0)

    total = jnp.sum(holder_counts[0])
    hold_rows = miss_slots.shape[1]
    live = jnp.arange(hold_rows, dtype=jnp.int32) < total
    held_slots = jnp.where(live, miss_slots[0], -1)
    all_slots = copy_for_each(held_slots, "narrow").reshape(narrow_count * hold_rows)
    all_rows = copy_for_each(miss_rows[0], "narrow").reshape(narrow_count * hold_rows, width)
    targets = all_slots - position * slot_count
    placing = targets[None, :] == jnp.arange(slot_count, dtype=jnp.int32)[:, None]
    placed = jnp.dot(
        placing.astype(jnp.bfloat16), all_rows, preferred_element_type=jnp.float32
    )
    struck = jnp.any(placing, axis=1)
    cache_next = jnp.where(struck[:, None], placed.astype(jnp.bfloat16), cache_table)[None]
    return (top_hidden, logits, cache_next)


def solution(mesh):
    return jax.shard_map(
        body,
        mesh=mesh,
        in_specs=(
            P("wide", "narrow", None),
            P("wide", None, None),
            P("wide", None),
            P("wide", "narrow", None),
            P("wide", "narrow"),
            P("wide", "narrow"),
            P(None, "narrow"),
            P("narrow"),
            P("narrow", None),
            P("narrow"),
            P("narrow"),
        ),
        out_specs=(P("wide", "narrow"), P("wide"), P("wide", "narrow", None)),
        check_vma=False,
    )
```

time: 504 us -> 265 us (0.53)
  local copies, waits for them, and re-layouts: 252 us -> 7.91 us
  Pallas kernels: 0 us -> 57.2 us
  other arithmetic: 45 us -> 7.83 us
  waiting for transfers between devices: 124 us -> 113 us
    gather x3 -> x0, local copies, waits for them, and re-layouts: 238 us -> none  [the longest x2 230 us: pool_block(): gathered = jnp.take(cache_table, positions, axis=0).astype(jnp.float32)]
    pallas_call x0 -> x1, Pallas kernels: none -> 57.2 us  [pool_rows(): pl.pallas_call(functools.partial(pool_kernel, bag_size, rows, first, coun...]
    reduce_sum x4 -> x2, other arithmetic: 30.2 us -> 1.23 us  [the longest x1 0.63 us: body(): total = jnp.sum(holder_counts[0])]
    reduce_scatter x1, waiting for transfers between devices: 62.2 us -> 38.4 us  [body(): lax.psum_scatter(second_terms.astype(jnp.bfloat16), 'narrow', scatter_dim...]
    all_to_all x2 -> x4, waiting for transfers between devices: 13.8 us -> 29.2 us  [copy_for_each(): lax.all_to_all(jnp.broadcast_to(x[None], (length, *x.shape)), axis, 0, 0,...]
    all_to_all x2 -> x4, starting transfers between devices: 8.64 us -> 15.7 us  [copy_for_each(): lax.all_to_all(jnp.broadcast_to(x[None], (length, *x.shape)), axis, 0, 0,...]
    all_to_all x2 -> x0, starting transfers between devices: 6.9 us -> none  [the longest x1 3.47 us: body(): lax.all_to_all(slab_rows, 'narrow', split_axis=0, concat_axis=0, tiled=True)]
where the time goes in v1:
time: 265 us; the launch traced here: 263 us
  waiting for transfers between devices  113 us (43%)
  Pallas kernels  57.2 us (22%)
  blocking collectives  24 us (9%)
  matrix products  24 us (9%)
  starting transfers between devices  15.7 us (6%)
  between operations  14.2 us (5%)
  local copies, waits for them, and re-layouts  7.91 us (3%)
  other arithmetic  7.83 us (3%)
    pallas_call x1, Pallas kernels, pool_rows(): pl.pallas_call(functools.partial(pool_kernel, bag_size, rows, first, coun...  57.2 us
    all_gather x1, waiting for transfers between devices, body(): features = lax.all_gather(arrived, 'narrow', axis=1, tiled=True)  44.8 us
    reduce_scatter x1, waiting for transfers between devices, body(): lax.psum_scatter(second_terms.astype(jnp.bfloat16), 'narrow', scatter_dim...  38.4 us
    all_to_all x4, waiting for transfers between devices, copy_for_each(): lax.all_to_all(jnp.broadcast_to(x[None], (length, *x.shape)), axis, 0, 0,...  29.2 us
    all_to_all x1, blocking collectives, body(): lax.all_to_all(pooled, 'wide', split_axis=0, concat_axis=0, tiled=True)  24 us
    dot_general x1, matrix products, body(): jnp.dot(first_hidden, w_second, preferred_element_type=jnp.float32)  16.8 us
    all_to_all x4, starting transfers between devices, copy_for_each(): lax.all_to_all(jnp.broadcast_to(x[None], (length, *x.shape)), axis, 0, 0,...  15.7 us
    dot_general x1, matrix products, body(): jnp.dot(placing.astype(jnp.bfloat16), all_rows, preferred_element_type=jn...  6.86 us
  transfers between devices with their start and end apart: 6, of which 4 were waited for; matrix products, arithmetic and copies ran while one was open for 7% of the time, Pallas kernels for 0%

profile of v1, /device:TPU:0, one launch (start us, length us, event | category | flops | bytes accessed | tf_op | source)
XLA Modules:
  0.0 263.4 jit_solution(8969486187773552058)
XLA Ops:
  7.2 2.7 %broadcast_in_dim.53 = bf16[4,2048,128]{2,1,0:T(8,128)(2,1)} broadcast(bf16[2048,128]{1,0:T(8,128)(2,1)} %bitcast.55), dimensions={1,2} | broadcast | bytes 2621440 | tf_op jit(solution)/shard_map/broadcast_in_dim | solution.py:18
  9.9 5.4 %all-to-all-start = ((bf16[4,2048,128]{2,1,0:T(8,128)(2,1)}), bf16[4,2048,128]{2,1,0:T(8,128)(2,1)S(1)}, u32[]{:S(2)}, u32[]{:S(2)}) async-start(bf16[4,2048,128]{2,1,0:T(8,128)(2,1)} %broadcast_in_dim.53), calls=%async_computation | async-start | bytes 4194304 | tf_op jit(solution)/shard_map/all_to_all | solution.py:18
  15.2 1.9 reshape.57
  17.7 23.9 %all-to-all-done = bf16[4,2048,128]{2,1,0:T(8,128)(2,1)S(1)} async-done(((bf16[4,2048,128]{2,1,0:T(8,128)(2,1)}), bf16[4,2048,128]{2,1,0:T(8,128)(2,1)S(1)}, u32[]{:S(2)}, u32[]{:S(2)}) %all-to-all-start) | async-done | bytes 2097184 | tf_op jit(solution)/shard_map/all_to_all | solution.py:18
  41.6 57.2 %pool.1 = bf16[4096,128]{1,0:T(8,128)(2,1)S(1)} custom-call(s32[65536]{0:T(1024)S(1)} %bitcast.52, bf16[8192,128]{1,0:T(8,128)(2,1)S(1)} %bitcast.50), custom_call_target="tpu_custom_call" | custom-call | flops 6710886400 | bytes 2097152 | tf_op jit(solution)/shard_map/pool/pallas_call | solution.py:52
  98.8 24.0 %all_to_all.27 = bf16[32,128,128]{2,1,0:T(8,128)(2,1)} all-to-all(bf16[32,128,128]{2,1,0:T(8,128)(2,1)S(1)} %bitcast.51), channel_id=1, replica_groups=mesh['wide'=32,'narrow'=4] {'wide'}, dimensions={0} | all-to-all | bytes 2097152 | tf_op jit(solution)/shard_map/all_to_all | solution.py:113
  122.9 44.8 %all-gather.2.cloned.1.call-done = bf16[32,512,128]{2,1,0:T(8,128)(2,1)} async-done(((bf16[32,128,128]{2,1,0:T(8,128)(2,1)}), bf16[32,512,128]{2,1,0:T(8,128)(2,1)}) %all-gather.2.cloned.1.call-update) | async-done | bytes 4194320 | tf_op jit(solution)/shard_map/all_gather | solution.py:114
  167.7 16.8 %convolution_convert_fusion = bf16[512,4096]{1,0:T(8,128)(2,1)} fusion(bf16[1024,4096]{1,0:T(8,128)(2,1)} %param.19, bf16[32,512,128]{2,1,0:T(8,128)(2,1)} %all-gather.2.cloned.1.call-done, bf16[32,128,1024]{2,1,0:T(8,128)(2,1)} %bitcast.62, f32[1024]{0:T(1024)S(1)} %copy-done.7), kind=kOutput, calls=%fused_computation.4 | convolution fusion | flops 8593604608 | bytes 25169920 | tf_op jit(solution)/shard_map/dot_general | solution.py:119
  184.5 0.6 copy-done.8
  185.1 0.6 reduce_sum.19
  185.8 0.7 compare_select_fusion
  186.4 0.6 broadcast_in_dim.56
  187.0 3.4 %all-to-all-start.3 = ((s32[4,1,1024]{2,1,0:T(1,128)}), s32[4,1,1024]{2,1,0:T(1,128)S(1)}, u32[]{:S(2)}, u32[]{:S(2)}) async-start(s32[4,1,1024]{2,1,0:T(1,128)} %broadcast_in_dim.56), calls=%async_computation.4 | async-start | bytes 32768 | tf_op jit(solution)/shard_map/all_to_all | solution.py:18
  190.4 5.4 %all-to-all-done.3 = s32[4,1,1024]{2,1,0:T(1,128)S(1)} async-done(((s32[4,1,1024]{2,1,0:T(1,128)}), s32[4,1,1024]{2,1,0:T(1,128)S(1)}, u32[]{:S(2)}, u32[]{:S(2)}) %all-to-all-start.3) | async-done | bytes 16416 | tf_op jit(solution)/shard_map/all_to_all | solution.py:18
  195.8 1.1 broadcast_in_dim.59
  196.9 3.5 %all-to-all-start.4 = ((bf16[4,1024,128]{2,1,0:T(8,128)(2,1)}), bf16[4,1024,128]{2,1,0:T(8,128)(2,1)S(1)}, u32[]{:S(2)}, u32[]{:S(2)}) async-start(bf16[4,1024,128]{2,1,0:T(8,128)(2,1)} %broadcast_in_dim.59), calls=%async_computation.5 | async-start | bytes 2097152 | tf_op jit(solution)/shard_map/all_to_all | solution.py:18
  200.4 4.3 %fusion.1 = pred[2048]{0:T(1024)(128)(4,1)S(1)} fusion(s32[4096]{0:T(1024)S(1)} %bitcast.59), kind=kLoop, calls=%fused_computation.2 | loop fusion | flops 16775168 | bytes 18432 | tf_op jit(solution)/shard_map/reduce_or | solution.py:141
  204.7 38.4 %reduce-scatter.2.cloned.1.call-done = bf16[512,1024]{1,0:T(8,128)(2,1)} async-done(((bf16[512,4096]{1,0:T(8,128)(2,1)}), bf16[512,1024]{1,0:T(8,128)(2,1)}) %reduce-scatter.2.cloned.1.call-update) | async-done | bytes 1048592 | tf_op jit(solution)/shard_map/reduce_scatter | solution.py:120
  243.2 1.5 maximum_convert_fusion
  244.7 0.4 fusion.9
  245.0 0.6 broadcast_in_dim.54
  245.7 3.4 %all-to-all-start.2 = ((f32[4,1,512]{2,1,0:T(1,128)}), f32[4,1,512]{2,1,0:T(1,128)S(1)}, u32[]{:S(2)}, u32[]{:S(2)}) async-start(f32[4,1,512]{2,1,0:T(1,128)} %broadcast_in_dim.54), calls=%async_computation.3 | async-start | bytes 16384 | tf_op jit(solution)/shard_map/all_to_all | solution.py:18
  249.1 6.9 %fusion.5 = bf16[1,2048,128]{2,1,0:T(8,128)(2,1)} fusion(bf16[4096,128]{1,0:T(8,128)(2,1)S(1)} %bitcast.54, s32[4096]{0:T(1024)S(1)} %bitcast.60, pred[2048]{0:T(1024)(128)(4,1)S(1)} %fusion.1, bf16[1,2048,128]{2,1,0:T(8,128)(2,1)S(1)} %copy-done.2), kind=kOutput, calls=%fused_computation.7 | convolution fusion | flops 2156396544 | bytes 2115584 | tf_op jit(solution)/shard_map/dot_general | solution.py:138
  255.9 0.6 reduce_sum.18
  (28 shorter events, 0.6 us)
Async XLA Ops:
  7.2 10.0 %copy-start = (s32[1,16384]{1,0:T(1,128)S(1)}, s32[1,16384]{1,0:T(1,128)}, u32[]{:S(2)}) copy-start(s32[1,16384]{1,0:T(1,128)} %param.13) | copy-start | bytes 196612
  9.9 31.7 %all-to-all-start = ((bf16[4,2048,128]{2,1,0:T(8,128)(2,1)}), bf16[4,2048,128]{2,1,0:T(8,128)(2,1)S(1)}, u32[]{:S(2)}, u32[]{:S(2)}) async-start(bf16[4,2048,128]{2,1,0:T(8,128)(2,1)} %broadcast_in_dim.53), calls=%async_computation | async-start | bytes 4194304 | tf_op jit(solution)/shard_map/all_to_all | solution.py:18
  15.2 152.5 %all-gather.2.cloned.1.call-start = ((), (), s32[]{:S(2)}) async-start(), calls=%async_computation.6 | async-start | bytes 5242880 | tf_op jit(solution)/shard_map/all_gather | solution.py:114
  41.6 126.1 %copy-start.7 = (f32[1024]{0:T(1024)S(1)}, f32[1024]{0:T(1024)}, u32[]{:S(2)}) copy-start(f32[1024]{0:T(1024)} %param.18) | copy-start | bytes 12292
  122.9 120.3 %reduce-scatter.2.cloned.1.call-start = ((), (), s32[]{:S(2)}) async-start(), calls=%async_computation.7 | async-start | bytes 5242880 | tf_op jit(solution)/shard_map/reduce_scatter | solution.py:120
  184.5 0.7 copy-start.8
  184.5 1.3 copy-start.5
  184.5 5.9 %copy-start.6 = (bf16[1024]{0:T(1024)(128)(2,1)S(1)}, bf16[1024]{0:T(1024)(128)(2,1)}, u32[]{:S(2)}) copy-start(bf16[1024]{0:T(1024)(128)(2,1)} %param.21) | copy-start | bytes 6148
  184.5 11.3 %copy-start.3 = (bf16[1,1024,128]{2,1,0:T(8,128)(2,1)S(1)}, bf16[1,1024,128]{2,1,0:T(8,128)(2,1)}, u32[]{:S(2)}) copy-start(bf16[1,1024,128]{2,1,0:T(8,128)(2,1)} %param.14) | copy-start | bytes 786436
  184.5 58.7 %copy-start.4 = (f32[1024]{0:T(1024)S(1)}, f32[1024]{0:T(1024)}, u32[]{:S(2)}) copy-start(f32[1024]{0:T(1024)} %param.20) | copy-start | bytes 12292
  185.1 64.0 %copy-start.2 = (bf16[1,2048,128]{2,1,0:T(8,128)(2,1)S(1)}, bf16[1,2048,128]{2,1,0:T(8,128)(2,1)}, u32[]{:S(2)}) copy-start(bf16[1,2048,128]{2,1,0:T(8,128)(2,1)} %param.11) | copy-start | bytes 1572868
  187.0 8.7 %all-to-all-start.3 = ((s32[4,1,1024]{2,1,0:T(1,128)}), s32[4,1,1024]{2,1,0:T(1,128)S(1)}, u32[]{:S(2)}, u32[]{:S(2)}) async-start(s32[4,1,1024]{2,1,0:T(1,128)} %broadcast_in_dim.56), calls=%async_computation.4 | async-start | bytes 32768 | tf_op jit(solution)/shard_map/all_to_all | solution.py:18
  196.9 48.1 %all-to-all-start.4 = ((bf16[4,1024,128]{2,1,0:T(8,128)(2,1)}), bf16[4,1024,128]{2,1,0:T(8,128)(2,1)S(1)}, u32[]{:S(2)}, u32[]{:S(2)}) async-start(bf16[4,1024,128]{2,1,0:T(8,128)(2,1)} %broadcast_in_dim.59), calls=%async_computation.5 | async-start | bytes 2097152 | tf_op jit(solution)/shard_map/all_to_all | solution.py:18
  244.7 11.3 %copy-start.1 = (bf16[512,1024]{1,0:T(8,128)(2,1)}, bf16[512,1024]{1,0:T(8,128)(2,1)S(1)}, u32[]{:S(2)}) copy-start(bf16[512,1024]{1,0:T(8,128)(2,1)S(1)} %maximum_convert_fusion) | copy-start | bytes 3145732
  245.7 10.3 %all-to-all-start.2 = ((f32[4,1,512]{2,1,0:T(1,128)}), f32[4,1,512]{2,1,0:T(1,128)S(1)}, u32[]{:S(2)}, u32[]{:S(2)}) async-start(f32[4,1,512]{2,1,0:T(1,128)} %broadcast_in_dim.54), calls=%async_computation.3 | async-start | bytes 16384 | tf_op jit(solution)/shard_map/all_to_all | solution.py:18
Sparse Core Ops, SparseCore 0:
  123.0 44.6 all-gather.1
  184.6 58.4 reduce-scatter.1

commit v2 on v1

v2 whole, which is shorter than its diff:
```python
import functools

import jax
import jax.numpy as jnp
from jax import lax
from jax.experimental import pallas as pl
from jax.experimental.pallas import tpu as pltpu
from jax.sharding import PartitionSpec as P

CHUNKS = 4
PAD = 16
UNROLL = 16
TILE = 256
MESH = pl.DeviceIdType.MESH


def copy_for_each(x, axis):
    length = lax.axis_size(axis)
    return lax.all_to_all(jnp.broadcast_to(x[None], (length, *x.shape)), axis, 0, 0, tiled=True)


def top_kernel(
    bag_size,
    wide_count,
    index_ref,
    cache_ref,
    w_first_hbm,
    b_first_ref,
    w_second_hbm,
    b_second_ref,
    top_ref,
    table,
    wide_table,
    pooled,
    sums,
    features,
    hidden,
    w_first,
    w_second,
    own_part,
    right_part,
    left_part,
    far_out,
    far_in,
    near_out,
    near_in,
    weight_sem,
    table_send,
    table_recv,
    exchange_send,
    exchange_recv,
    gather_send,
    gather_recv,
    pass_send,
    pass_recv,
    far_send,
    far_recv,
    near_send,
    near_recv,
):
    me = lax.axis_index("wide")
    place = lax.axis_index("narrow")
    right, left = lax.rem(place + 1, 4), lax.rem(place + 3, 4)
    slots, width = cache_ref.shape
    chunks, block, _ = features.shape
    rows = pooled.shape[1]
    count = rows // chunks
    owner_rows = top_ref.shape[0] // 4
    sides = ((0, right), (1, left))

    first_copy = pltpu.make_async_copy(w_first_hbm, w_first, weight_sem.at[0])
    second_copy = pltpu.make_async_copy(w_second_hbm, w_second, weight_sem.at[1])
    first_copy.start()
    second_copy.start()

    barrier = pltpu.get_barrier_semaphore()

    def greet(i, _):
        pl.semaphore_signal(
            barrier, inc=1, device_id={"wide": lax.rem(me + i, wide_count)}, device_id_type=MESH
        )
        return 0

    lax.fori_loop(1, wide_count, greet, 0)
    for _, other in sides:
        pl.semaphore_signal(barrier, inc=1, device_id={"narrow": other}, device_id_type=MESH)
    pl.semaphore_wait(barrier, wide_count + 1)

    def to_side(source, target, send, recv, other):
        return pltpu.make_async_remote_copy(
            src_ref=source,
            dst_ref=target,
            send_sem=send,
            recv_sem=recv,
            device_id={"narrow": other},
            device_id_type=MESH,
        )

    half = slots // 2
    near_tables = [
        to_side(cache_ref, table.at[place], table_send.at[k], table_recv.at[k], other)
        for k, other in sides
    ]
    for copy in near_tables:
        copy.start()
    wide_table[pl.ds(pl.multiple_of(place * slots, slots), slots), :] = cache_ref[...].astype(jnp.float32)
    wide_table[4 * slots :, :] = jnp.zeros((PAD, width), jnp.float32)
    far_tables = []
    for k, other, source in ((0, right, left), (1, left, right)):
        near_tables[k].wait_recv()
        part = table.at[source, pl.ds(k * half, half)]
        copy = to_side(part, part, table_send.at[2 + k], table_recv.at[2 + k], other)
        copy.start()
        far_tables.append(copy)

    def widen(source):
        wide_table[pl.ds(pl.multiple_of(source * slots, slots), slots), :] = table[source].astype(jnp.float32)

    widen(left)
    widen(right)
    for copy in far_tables:
        copy.wait_recv()
    widen(lax.rem(place + 2, 4))
    for copy in near_tables + far_tables:
        copy.wait_send()

    def pool(chunk, low, high):
        def owner_step(i, _):
            owner = lax.rem(me + i, wide_count)
            base = owner * (bag_size * rows) + chunk * count

            def row_step(j, _):
                for u in range(UNROLL):
                    terms = [
                        wide_table[pl.ds(index_ref[base + j * UNROLL + (l * rows + u)], 1), :]
                        for l in range(bag_size)
                    ]
                    while len(terms) > 1:
                        terms = [terms[k] + terms[k + 1] for k in range(0, len(terms), 2)]
                    sums[pl.ds(j * UNROLL + u, 1), :] = terms[0]
                return 0

            lax.fori_loop(0, count // UNROLL, row_step, 0)
            source = pooled.at[owner, pl.ds(chunk * count, count)]
            source[...] = sums[...].astype(jnp.bfloat16)
            target = features.at[
                chunk,
                pl.ds(pl.multiple_of(place * count, count), count),
                pl.ds(pl.multiple_of(me * width, width), width),
            ]

            @pl.when(i == 0)
            def _():
                pltpu.make_async_copy(source, target, exchange_recv.at[chunk]).start()

            @pl.when(i > 0)
            def _():
                pltpu.make_async_remote_copy(
                    src_ref=source,
                    dst_ref=target,
                    send_sem=exchange_send.at[chunk],
                    recv_sem=exchange_recv.at[chunk],
                    device_id={"wide": owner},
                    device_id_type=MESH,
                ).start()

            return 0

        lax.fori_loop(low, high, owner_step, 0)

    def own_rows(chunk, source, low, length):
        return features.at[chunk, pl.ds(pl.multiple_of(source * count + low, 16), length)]

    def near_copies(chunk):
        part = own_rows(chunk, place, 0, count)
        return [
            to_side(part, part, gather_send.at[chunk, k], gather_recv.at[chunk, k], other)
            for k, other in sides
        ]

    def pass_copies(chunk):
        part = count // 2
        found = []
        for k, other, source in ((0, right, left), (1, left, right)):
            view = own_rows(chunk, source, k * part, part)
            found.append(to_side(view, view, pass_send.at[chunk, k], pass_recv.at[chunk, k], other))
        return found

    def far_copies(chunk):
        return [
            to_side(far_out.at[chunk, k], far_in.at[chunk, k], far_send.at[chunk, k], far_recv.at[chunk, k], other)
            for k, other in sides
        ]

    def near_sums(chunk):
        return [
            to_side(near_out.at[chunk, k], near_in.at[chunk, k], near_send.at[chunk, k], near_recv.at[chunk, k], other)
            for k, other in sides
        ]

    def exchanged(chunk):
        whole = own_rows(chunk, place, 0, count)
        pltpu.make_async_copy(whole, whole, exchange_recv.at[chunk]).wait()
        for copy in near_copies(chunk):
            copy.start()

    def pass_on(chunk):
        for near, on in zip(near_copies(chunk), pass_copies(chunk)):
            near.wait_recv()
            on.start()

    middle = block // 2
    columns = top_ref.shape[1]

    def layers(chunk):
        for copy in pass_copies(chunk):
            copy.wait_recv()
        if chunk == 0:
            first_copy.wait()
            second_copy.wait()

        def first(t, _):
            span = pl.ds(pl.multiple_of(t * TILE, TILE), TILE)
            terms = jnp.dot(features[chunk], w_first[:, span], preferred_element_type=jnp.float32)
            hidden[:, span] = jnp.maximum(terms + b_first_ref[:, span], 0.0).astype(jnp.bfloat16)
            return 0

        lax.fori_loop(0, columns // TILE, first, 0)

        def second(ahead, keep):
            target = lax.rem(place + ahead, 4)

            def step(t, _):
                span = pl.ds(pl.multiple_of(t * TILE, TILE), TILE)
                from_ = pl.ds(pl.multiple_of(target * columns + t * TILE, TILE), TILE)
                keep(span, jnp.dot(hidden[...], w_second[:, from_], preferred_element_type=jnp.float32))
                return 0

            lax.fori_loop(0, columns // TILE, step, 0)

        def keep_far(span, terms):
            far_out[chunk, 0, :, span] = terms[:middle].astype(jnp.bfloat16)
            far_out[chunk, 1, :, span] = terms[middle:].astype(jnp.bfloat16)

        second(2, keep_far)
        for copy in far_copies(chunk):
            copy.start()

        def keep_right(span, terms):
            right_part[:, span] = terms

        def keep_left(span, terms):
            left_part[:, span] = terms

        def keep_own(span, terms):
            own_part[chunk, :, span] = terms

        second(1, keep_right)
        second(3, keep_left)
        second(0, keep_own)

    def join(chunk):
        parts = (right_part, left_part)
        for k, copy in enumerate(far_copies(chunk)):
            copy.wait_recv()
            summed = pl.ds(k * middle, middle)
            alone = pl.ds((1 - k) * middle, middle)
            near_out[chunk, k, summed, :] = (
                parts[k][summed, :] + far_in[chunk, k].astype(jnp.float32)
            ).astype(jnp.bfloat16)
            near_out[chunk, k, alone, :] = parts[k][alone, :].astype(jnp.bfloat16)
        for copy in near_sums(chunk):
            copy.start()

    def finish(chunk):
        for copy in near_sums(chunk):
            copy.wait_recv()
        terms = own_part[chunk] + near_in[chunk, 0].astype(jnp.float32) + near_in[chunk, 1].astype(jnp.float32)
        top = jnp.maximum(terms + b_second_ref[...], 0.0).astype(jnp.bfloat16)
        for q in range(4):
            top_ref[pl.ds(q * owner_rows + chunk * count, count), :] = top[q * count : (q + 1) * count]

    part = wide_count // 2
    for chunk in range(chunks + 1):
        for half_step in range(2):
            if chunk < chunks:
                pool(chunk, half_step * part, (half_step + 1) * part)
            if half_step == 0:
                if chunk >= 1:
                    exchanged(chunk - 1)
                if chunk >= 2:
                    layers(chunk - 2)
            else:
                if chunk >= 1:
                    pass_on(chunk - 1)
                if chunk >= 2:
                    join(chunk - 2)
                if chunk >= 3:
                    finish(chunk - 3)
    layers(chunks - 1)
    if chunks >= 2:
        finish(chunks - 2)
    join(chunks - 1)
    finish(chunks - 1)

    for chunk in range(chunks):
        sent = pooled.at[pl.ds(0, wide_count - 1), pl.ds(0, count)]
        pltpu.make_async_copy(sent, sent, exchange_send.at[chunk]).wait()
        for copies in (near_copies, pass_copies, far_copies, near_sums):
            for copy in copies(chunk):
                copy.wait_send()


def top_network(indices, cache_table, w_first, b_first, w_second, b_second, bag_size, wide_count):
    slots, width = cache_table.shape
    rows = indices.shape[0] // (bag_size * wide_count)
    count = rows // CHUNKS
    block = 4 * count
    fan_in, columns = w_first.shape
    vmem = pl.BlockSpec(memory_space=pltpu.VMEM)
    hbm = pl.BlockSpec(memory_space=pl.ANY)
    pairs = [pltpu.SemaphoreType.DMA((CHUNKS, 2))] * 8
    return pl.pallas_call(
        functools.partial(top_kernel, bag_size, wide_count),
        out_shape=jax.ShapeDtypeStruct((4 * rows, columns), jnp.bfloat16),
        in_specs=[pl.BlockSpec(memory_space=pltpu.SMEM), vmem, hbm, vmem, hbm, vmem],
        out_specs=vmem,
        scratch_shapes=[
            pltpu.VMEM((4, slots, width), jnp.bfloat16),
            pltpu.VMEM((4 * slots + PAD, width), jnp.float32),
            pltpu.VMEM((wide_count, rows, width), jnp.bfloat16),
            pltpu.VMEM((count, width), jnp.float32),
            pltpu.VMEM((CHUNKS, block, fan_in), jnp.bfloat16),
            pltpu.VMEM((block, columns), jnp.bfloat16),
            pltpu.VMEM((fan_in, columns), jnp.bfloat16),
            pltpu.VMEM((columns, fan_in), jnp.bfloat16),
            pltpu.VMEM((CHUNKS, block, columns), jnp.float32),
            pltpu.VMEM((block, columns), jnp.float32),
            pltpu.VMEM((block, columns), jnp.float32),
            pltpu.VMEM((CHUNKS, 2, block // 2, columns), jnp.bfloat16),
            pltpu.VMEM((CHUNKS, 2, block // 2, columns), jnp.bfloat16),
            pltpu.VMEM((CHUNKS, 2, block, columns), jnp.bfloat16),
            pltpu.VMEM((CHUNKS, 2, block, columns), jnp.bfloat16),
            pltpu.SemaphoreType.DMA((2,)),
            pltpu.SemaphoreType.DMA((4,)),
            pltpu.SemaphoreType.DMA((4,)),
            pltpu.SemaphoreType.DMA((CHUNKS,)),
            pltpu.SemaphoreType.DMA((CHUNKS,)),
            *pairs,
        ],
        compiler_params=pltpu.CompilerParams(
            collective_id=1, has_side_effects=True, vmem_limit_bytes=56 << 20
        ),
        cost_estimate=pl.CostEstimate(
            flops=4 * 4 * rows * fan_in * columns,
            bytes_accessed=2 * 2 * fan_in * columns,
            transcendentals=0,
        ),
        name="top_network",
    )(indices, cache_table, w_first, b_first[None], w_second, b_second[None])


def body(
    cache,
    lookup_slots,
    bag_lengths,
    miss_rows,
    miss_slots,
    holder_counts,
    w_first,
    b_first,
    w_second,
    b_second,
    w_out,
):
    wide_count = lax.axis_size("wide")
    narrow_count = lax.axis_size("narrow")
    position = lax.axis_index("narrow")
    cache_table = cache[0]
    slot_count, width = cache_table.shape
    batch_rows, bag_size = lookup_slots.shape[1:]
    owner_rows = batch_rows // wide_count
    rows = owner_rows // narrow_count

    by_lookup = lookup_slots[0].T.reshape(bag_size, wide_count, narrow_count, rows)
    by_lookup = lax.dynamic_index_in_dim(by_lookup, position, 2, keepdims=False)
    lengths = bag_lengths[0].reshape(wide_count, narrow_count, rows)
    lengths = lax.dynamic_index_in_dim(lengths, position, 1, keepdims=False)
    used = jnp.arange(bag_size, dtype=jnp.int32)[:, None, None] < lengths[None]
    indices = jnp.where(used, by_lookup, narrow_count * slot_count)
    indices = indices.transpose(1, 0, 2).reshape(wide_count * bag_size * rows)

    top_hidden = top_network(
        indices, cache_table, w_first, b_first, w_second, b_second, bag_size, wide_count
    )
    logit_term = jnp.dot(top_hidden, w_out, preferred_element_type=jnp.float32)
    logits = jnp.sum(copy_for_each(logit_term, "narrow"), axis=0)

    total = jnp.sum(holder_counts[0])
    hold_rows = miss_slots.shape[1]
    live = jnp.arange(hold_rows, dtype=jnp.int32) < total
    held_slots = jnp.where(live, miss_slots[0], -1)
    all_slots = copy_for_each(held_slots, "narrow").reshape(narrow_count * hold_rows)
    all_rows = copy_for_each(miss_rows[0], "narrow").reshape(narrow_count * hold_rows, width)
    targets = all_slots - position * slot_count
    placing = targets[None, :] == jnp.arange(slot_count, dtype=jnp.int32)[:, None]
    placed = jnp.dot(
        placing.astype(jnp.bfloat16), all_rows, preferred_element_type=jnp.float32
    )
    struck = jnp.any(placing, axis=1)
    cache_next = jnp.where(struck[:, None], placed.astype(jnp.bfloat16), cache_table)[None]
    return (top_hidden, logits, cache_next)


def solution(mesh):
    return jax.shard_map(
        body,
        mesh=mesh,
        in_specs=(
            P("wide", "narrow", None),
            P("wide", None, None),
            P("wide", None),
            P("wide", "narrow", None),
            P("wide", "narrow"),
            P("wide", "narrow"),
            P(None, "narrow"),
            P("narrow"),
            P("narrow", None),
            P("narrow"),
            P("narrow"),
        ),
        out_specs=(P("wide", "narrow"), P("wide"), P("wide", "narrow", None)),
        check_vma=False,
    )
```

time: 265 us -> 191 us (0.72)
  waiting for transfers between devices: 113 us -> 9.82 us
  Pallas kernels: 57.2 us -> 144 us
  blocking collectives: 24 us -> 7.71 us
  matrix products: 24 us -> 8.44 us
  between operations: 14.2 us -> 0.72 us
  starting transfers between devices: 15.7 us -> 7.76 us
    pallas_call x1, Pallas kernels: 57.2 us -> 144 us  [top_network(): pl.pallas_call(functools.partial(top_kernel, bag_size, wide_count), out_s...]
    all_gather x1 -> x0, waiting for transfers between devices: 44.8 us -> none  [body(): features = lax.all_gather(arrived, 'narrow', axis=1, tiled=True)]
    reduce_scatter x1 -> x0, waiting for transfers between devices: 38.4 us -> none  [body(): lax.psum_scatter(second_terms.astype(jnp.bfloat16), 'narrow', scatter_dim...]
    all_to_all x4 -> x2, waiting for transfers between devices: 29.2 us -> 9.82 us  [copy_for_each(): lax.all_to_all(jnp.broadcast_to(x[None], (length, *x.shape)), axis, 0, 0,...]
    all_to_all x1, blocking collectives: 24 us -> 7.71 us  [copy_for_each(): lax.all_to_all(jnp.broadcast_to(x[None], (length, *x.shape)), axis, 0, 0,...]
    dot_general x2 -> x1, matrix products: 17.1 us -> 1.6 us  [body(): logit_term = jnp.dot(top_hidden, w_out, preferred_element_type=jnp.float32)]
    all_to_all x4 -> x2, starting transfers between devices: 15.7 us -> 7.76 us  [copy_for_each(): lax.all_to_all(jnp.broadcast_to(x[None], (length, *x.shape)), axis, 0, 0,...]
    broadcast_in_dim x4 -> x3, local copies, waits for them, and re-layouts: 5.03 us -> 1.74 us  [copy_for_each(): jnp.broadcast_to(x[None], (length, *x.shape))]
  transfers between devices with their start and end apart: 6 -> 2, of which waited for: 4 -> 2; matrix products, arithmetic and copies ran while one was open for 7% -> 3% of each run, Pallas kernels for 0% -> 0%
where the time goes in v2:
time: 191 us
  Pallas kernels  144 us (75%)
  waiting for transfers between devices  9.82 us (5%)
  matrix products  8.44 us (4%)
  starting transfers between devices  7.76 us (4%)
  blocking collectives  7.71 us (4%)
  other arithmetic  7.04 us (4%)
  local copies, waits for them, and re-layouts  5.68 us (3%)
    pallas_call x1, Pallas kernels, top_network(): pl.pallas_call(functools.partial(top_kernel, bag_size, wide_count), out_s...  144 us
    all_to_all x2, waiting for transfers between devices, copy_for_each(): lax.all_to_all(jnp.broadcast_to(x[None], (length, *x.shape)), axis, 0, 0,...  9.82 us
    all_to_all x2, starting transfers between devices, copy_for_each(): lax.all_to_all(jnp.broadcast_to(x[None], (length, *x.shape)), axis, 0, 0,...  7.76 us
    all_to_all x1, blocking collectives, copy_for_each(): lax.all_to_all(jnp.broadcast_to(x[None], (length, *x.shape)), axis, 0, 0,...  7.71 us
    dot_general x1, matrix products, body(): jnp.dot(placing.astype(jnp.bfloat16), all_rows, preferred_element_type=jn...  6.85 us
    reduce_or x1, other arithmetic, body(): struck = jnp.any(placing, axis=1)  4.26 us
  transfers between devices with their start and end apart: 2, of which 2 were waited for; matrix products, arithmetic and copies ran while one was open for 3% of the time, Pallas kernels for 0%

profile of v2, /device:TPU:0, one launch (start us, length us, event | category | flops | bytes accessed | tf_op | source)
XLA Modules:
  0.0 190.8 jit_solution(8109157462823937509)
XLA Ops:
  0.6 0.0 copy-start
  0.6 2.0 %reshape.46 = s32[16,32,4,128]{3,2,1,0:T(4,128)S(1)} reshape(s32[16,16384]{1,0:T(8,128)} %bitcast.27) | data formatting | bytes 2097152 | tf_op jit(solution)/shard_map/reshape | solution.py:385
  2.6 0.3 constant_dynamic-slice_fusion
  2.9 0.0 copy-done
  2.9 0.7 reshape.49
  3.6 0.9 fusion.6
  4.5 143.6 %top_network.1 = bf16[512,1024]{1,0:T(8,128)(2,1)} custom-call(s32[65536]{0:T(1024)} %bitcast.30, bf16[2048,128]{1,0:T(8,128)(2,1)} %bitcast.36, bf16[4096,1024]{1,0:T(8,128)(2,1)} %w_first_hbm.1, f32[1,1024]{1,0:T(1,128)} %bitcast.37, bf16[1024,4096]{1,0:T(8,128)(2,1)} %w_second_hbm.1, f32[1,1024]{1,0:T(1,128)} %bitcast.38), custom_call_target="tpu_custom_call" | custom-call | flops 8589934592 | bytes 16777216 | tf_op jit(solution)/shard_map/top_network/pallas_call | solution.py:323
  148.1 1.6 fusion.7
  149.7 0.6 broadcast_in_dim.52
  150.3 4.1 %all-to-all-start = ((f32[4,1,512]{2,1,0:T(1,128)}), f32[4,1,512]{2,1,0:T(1,128)S(1)}, u32[]{:S(2)}, u32[]{:S(2)}) async-start(f32[4,1,512]{2,1,0:T(1,128)} %broadcast_in_dim.52), calls=%async_computation | async-start | bytes 16384 | tf_op jit(solution)/shard_map/all_to_all | solution.py:19
  154.4 0.0 copy-done.5
  154.4 0.6 reduce_sum.19
  155.0 0.0 copy-done.3
  155.0 0.7 compare_select_fusion
  155.7 4.0 %all-to-all-done = f32[4,1,512]{2,1,0:T(1,128)S(1)} async-done(((f32[4,1,512]{2,1,0:T(1,128)}), f32[4,1,512]{2,1,0:T(1,128)S(1)}, u32[]{:S(2)}, u32[]{:S(2)}) %all-to-all-start) | async-done | bytes 8224 | tf_op jit(solution)/shard_map/all_to_all | solution.py:19
  159.7 7.7 %all_to_all.17 = s32[4,1,1024]{2,1,0:T(1,128)S(1)} all-to-all(s32[4,1,1024]{2,1,0:T(1,128)S(1)} %broadcast_in_dim.54), channel_id=1, replica_groups=mesh['wide'=32,'narrow'=4] {'narrow'}, dimensions={0} | all-to-all | bytes 32768 | tf_op jit(solution)/shard_map/all_to_all | solution.py:19
  167.5 1.1 broadcast_in_dim.57
  168.6 3.7 %all-to-all-start.2 = ((bf16[4,1024,128]{2,1,0:T(8,128)(2,1)}), bf16[4,1024,128]{2,1,0:T(8,128)(2,1)S(1)}, u32[]{:S(2)}, u32[]{:S(2)}) async-start(bf16[4,1024,128]{2,1,0:T(8,128)(2,1)} %broadcast_in_dim.57), calls=%async_computation.2 | async-start | bytes 2097152 | tf_op jit(solution)/shard_map/all_to_all | solution.py:19
  172.3 0.6 reduce_sum.18
  172.9 4.3 %fusion.1 = pred[2048]{0:T(1024)(128)(4,1)S(1)} fusion(s32[4096]{0:T(1024)S(1)} %bitcast.33), kind=kLoop, calls=%fused_computation.2 | loop fusion | flops 16775168 | bytes 18432 | tf_op jit(solution)/shard_map/reduce_or | solution.py:410
  177.1 5.8 %all-to-all-done.2 = bf16[4,1024,128]{2,1,0:T(8,128)(2,1)S(1)} async-done(((bf16[4,1024,128]{2,1,0:T(8,128)(2,1)}), bf16[4,1024,128]{2,1,0:T(8,128)(2,1)S(1)}, u32[]{:S(2)}, u32[]{:S(2)}) %all-to-all-start.2) | async-done | bytes 1048608 | tf_op jit(solution)/shard_map/all_to_all | solution.py:19
  182.9 6.8 %fusion.5 = bf16[1,2048,128]{2,1,0:T(8,128)(2,1)} fusion(bf16[4096,128]{1,0:T(8,128)(2,1)S(1)} %bitcast.28, s32[4096]{0:T(1024)S(1)} %bitcast.34, pred[2048]{0:T(1024)(128)(4,1)S(1)} %fusion.1, bf16[1,2048,128]{2,1,0:T(8,128)(2,1)S(1)} %copy-done.4), kind=kOutput, calls=%fused_computation.6 | convolution fusion | flops 2156396544 | bytes 2115584 | tf_op jit(solution)/shard_map/dot_general | solution.py:407
  189.8 0.0 copy-done.1
  189.8 1.0 copy.24
  (10 shorter events, 0.1 us)
Async XLA Ops:
  0.6 2.3 %copy-start = (s32[1,16384]{1,0:T(1,128)S(1)}, s32[1,16384]{1,0:T(1,128)}, u32[]{:S(2)}) copy-start(s32[1,16384]{1,0:T(1,128)} %param.13) | copy-start | bytes 196612
  4.5 149.9 %copy-start.5 = (s32[1,4]{1,0:T(1,128)S(1)}, s32[1,4]{1,0:T(1,128)}, u32[]{:S(2)}) copy-start(s32[1,4]{1,0:T(1,128)} %param.16) | copy-start | bytes 52
  4.5 150.5 %copy-start.3 = (s32[1,1024]{1,0:T(1,128)S(1)}, s32[1,1024]{1,0:T(1,128)}, u32[]{:S(2)}) copy-start(s32[1,1024]{1,0:T(1,128)} %param.15) | copy-start | bytes 12292
  4.5 162.9 %copy-start.2 = (bf16[1,1024,128]{2,1,0:T(8,128)(2,1)S(1)}, bf16[1,1024,128]{2,1,0:T(8,128)(2,1)}, u32[]{:S(2)}) copy-start(bf16[1,1024,128]{2,1,0:T(8,128)(2,1)} %param.14) | copy-start | bytes 786436
  4.5 178.4 %copy-start.4 = (bf16[1,2048,128]{2,1,0:T(8,128)(2,1)S(1)}, bf16[1,2048,128]{2,1,0:T(8,128)(2,1)}, u32[]{:S(2)}) copy-start(bf16[1,2048,128]{2,1,0:T(8,128)(2,1)} %param.11) | copy-start | bytes 1572868
  150.3 9.4 %all-to-all-start = ((f32[4,1,512]{2,1,0:T(1,128)}), f32[4,1,512]{2,1,0:T(1,128)S(1)}, u32[]{:S(2)}, u32[]{:S(2)}) async-start(f32[4,1,512]{2,1,0:T(1,128)} %broadcast_in_dim.52), calls=%async_computation | async-start | bytes 16384 | tf_op jit(solution)/shard_map/all_to_all | solution.py:19
  168.6 14.4 %all-to-all-start.2 = ((bf16[4,1024,128]{2,1,0:T(8,128)(2,1)}), bf16[4,1024,128]{2,1,0:T(8,128)(2,1)S(1)}, u32[]{:S(2)}, u32[]{:S(2)}) async-start(bf16[4,1024,128]{2,1,0:T(8,128)(2,1)} %broadcast_in_dim.57), calls=%async_computation.2 | async-start | bytes 2097152 | tf_op jit(solution)/shard_map/all_to_all | solution.py:19
  182.9 6.9 %copy-start.1 = (bf16[512,1024]{1,0:T(8,128)(2,1)S(1)}, bf16[512,1024]{1,0:T(8,128)(2,1)}, u32[]{:S(2)}) copy-start(bf16[512,1024]{1,0:T(8,128)(2,1)} %top_network.1) | copy-start | bytes 3145732

commit v3 on v2

--- a/solution.py
+++ b/solution.py
@@ -12,11 +12,6 @@
 UNROLL = 16
 TILE = 256
 MESH = pl.DeviceIdType.MESH
-
-
-def copy_for_each(x, axis):
-    length = lax.axis_size(axis)
-    return lax.all_to_all(jnp.broadcast_to(x[None], (length, *x.shape)), axis, 0, 0, tiled=True)
 
 
 def top_kernel(
@@ -28,7 +23,13 @@
     b_first_ref,
     w_second_hbm,
     b_second_ref,
+    w_out_ref,
+    miss_rows_ref,
+    miss_slots_ref,
+    counts_ref,
     top_ref,
+    logits_ref,
+    cache_next_ref,
     table,
     wide_table,
     pooled,
@@ -44,6 +45,9 @@
     far_in,
     near_out,
     near_in,
+    held_rows,
+    held_slots,
+    logit_parts,
     weight_sem,
     table_send,
     table_recv,
@@ -57,6 +61,12 @@
     far_recv,
     near_send,
     near_recv,
+    rows_send,
+    rows_recv,
+    slots_send,
+    slots_recv,
+    logit_send,
+    logit_recv,
 ):
     me = lax.axis_index("wide")
     place = lax.axis_index("narrow")
@@ -67,6 +77,8 @@
     count = rows // chunks
     owner_rows = top_ref.shape[0] // 4
     sides = ((0, right), (1, left))
+    opposite = lax.rem(place + 2, 4)
+    everyone = ((0, right), (1, left), (2, opposite))
 
     first_copy = pltpu.make_async_copy(w_first_hbm, w_first, weight_sem.at[0])
     second_copy = pltpu.make_async_copy(w_second_hbm, w_second, weight_sem.at[1])
@@ -82,9 +94,17 @@
         return 0
 
     lax.fori_loop(1, wide_count, greet, 0)
-    for _, other in sides:
+    for _, other in everyone:
         pl.semaphore_signal(barrier, inc=1, device_id={"narrow": other}, device_id_type=MESH)
-    pl.semaphore_wait(barrier, wide_count + 1)
+
+    hold = miss_rows_ref.shape[0]
+    total = counts_ref[0] + counts_ref[1] + counts_ref[2] + counts_ref[3]
+    position = lax.broadcasted_iota(jnp.int32, (1, hold), 1)
+    held_slots[place] = jnp.where(position < total, miss_slots_ref[...], -1)
+    held_rows[:, :, width:] = jnp.ones((4, hold, width), jnp.bfloat16)
+    held_rows[place, :, :width] = miss_rows_ref[...]
+
+    pl.semaphore_wait(barrier, wide_count + 2)
 
     def to_side(source, target, send, recv, other):
         return pltpu.make_async_remote_copy(
@@ -120,9 +140,46 @@
     widen(right)
     for copy in far_tables:
         copy.wait_recv()
-    widen(lax.rem(place + 2, 4))
-    for copy in near_tables + far_tables:
-        copy.wait_send()
+    widen(opposite)
+
+    slot_copies = [
+        to_side(held_slots.at[place], held_slots.at[place], slots_send.at[k], slots_recv.at[k], other)
+        for k, other in everyone
+    ]
+    own_held = held_rows.at[place, :, pl.ds(0, width)]
+    near_held = [
+        to_side(own_held, own_held, rows_send.at[k], rows_recv.at[k], other) for k, other in sides
+    ]
+    for copy in slot_copies + near_held:
+        copy.start()
+    far_held = []
+    for k, other, source in ((0, right, left), (1, left, right)):
+        part = held_rows.at[source, pl.ds(k * (hold // 2), hold // 2), pl.ds(0, width)]
+        far_held.append(to_side(part, part, rows_send.at[2 + k], rows_recv.at[2 + k], other))
+
+    def pass_held():
+        for near, far in zip(near_held, far_held):
+            near.wait_recv()
+            far.start()
+
+    def held_arrived():
+        for copy in slot_copies + far_held:
+            copy.wait_recv()
+
+    def refill(low, high):
+        def step(t, _):
+            span = pl.ds(pl.multiple_of(t * TILE, TILE), TILE)
+            slot = place * slots + t * TILE + lax.broadcasted_iota(jnp.int32, (TILE, hold), 0)
+            placed = jnp.zeros((TILE, 2 * width), jnp.float32)
+            for q in range(4):
+                chosen = jnp.where(held_slots[q] == slot, 1.0, 0.0).astype(jnp.bfloat16)
+                placed += jnp.dot(chosen, held_rows[q], preferred_element_type=jnp.float32)
+            cache_next_ref[span, :] = jnp.where(
+                placed[:, width:] > 0.5, placed[:, :width].astype(jnp.bfloat16), cache_ref[span, :]
+            )
+            return 0
+
+        lax.fori_loop(low, high, step, 0)
 
     def pool(chunk, low, high):
         def owner_step(i, _):
@@ -281,37 +338,74 @@
             top_ref[pl.ds(q * owner_rows + chunk * count, count), :] = top[q * count : (q + 1) * count]
 
     part = wide_count // 2
+    blocks = slots // TILE
     for chunk in range(chunks + 1):
         for half_step in range(2):
             if chunk < chunks:
                 pool(chunk, half_step * part, (half_step + 1) * part)
             if half_step == 0:
+                if chunk == 0:
+                    pass_held()
                 if chunk >= 1:
                     exchanged(chunk - 1)
                 if chunk >= 2:
                     layers(chunk - 2)
             else:
+                if chunk == 0:
+                    held_arrived()
                 if chunk >= 1:
                     pass_on(chunk - 1)
                 if chunk >= 2:
                     join(chunk - 2)
                 if chunk >= 3:
                     finish(chunk - 3)
+    refill(0, blocks // 2)
     layers(chunks - 1)
-    if chunks >= 2:
-        finish(chunks - 2)
+    finish(chunks - 2)
     join(chunks - 1)
+    refill(blocks // 2, blocks)
     finish(chunks - 1)
 
+    logit_parts[place] = lax.dot_general(
+        w_out_ref[...], top_ref[...], (((1,), (1,)), ((), ())), preferred_element_type=jnp.float32
+    )[:8]
+    logit_copies = [
+        to_side(logit_parts.at[place], logit_parts.at[place], logit_send.at[k], logit_recv.at[k], other)
+        for k, other in everyone
+    ]
+    for copy in logit_copies:
+        copy.start()
     for chunk in range(chunks):
         sent = pooled.at[pl.ds(0, wide_count - 1), pl.ds(0, count)]
         pltpu.make_async_copy(sent, sent, exchange_send.at[chunk]).wait()
         for copies in (near_copies, pass_copies, far_copies, near_sums):
             for copy in copies(chunk):
                 copy.wait_send()
-
-
-def top_network(indices, cache_table, w_first, b_first, w_second, b_second, bag_size, wide_count):
+    for copy in near_tables + far_tables + slot_copies + near_held + far_held:
+        copy.wait_send()
+    for copy in logit_copies:
+        copy.wait_recv()
+    logits_ref[...] = (
+        logit_parts[0][:1] + logit_parts[1][:1] + (logit_parts[2][:1] + logit_parts[3][:1])
+    )
+    for copy in logit_copies:
+        copy.wait_send()
+
+
+def top_network(
+    indices,
+    cache_table,
+    w_first,
+    b_first,
+    w_second,
+    b_second,
+    w_out,
+    miss_rows,
+    miss_slots,
+    counts,
+    bag_size,
+    wide_count,
+):
     slots, width = cache_table.shape
     rows = indices.shape[0] // (bag_size * wide_count)
     count = rows // CHUNKS
@@ -319,12 +413,18 @@
     fan_in, columns = w_first.shape
     vmem = pl.BlockSpec(memory_space=pltpu.VMEM)
     hbm = pl.BlockSpec(memory_space=pl.ANY)
+    smem = pl.BlockSpec(memory_space=pltpu.SMEM)
+    hold = miss_rows.shape[0]
     pairs = [pltpu.SemaphoreType.DMA((CHUNKS, 2))] * 8
     return pl.pallas_call(
         functools.partial(top_kernel, bag_size, wide_count),
-        out_shape=jax.ShapeDtypeStruct((4 * rows, columns), jnp.bfloat16),
-        in_specs=[pl.BlockSpec(memory_space=pltpu.SMEM), vmem, hbm, vmem, hbm, vmem],
-        out_specs=vmem,
+        out_shape=(
+            jax.ShapeDtypeStruct((4 * rows, columns), jnp.bfloat16),
+            jax.ShapeDtypeStruct((1, 4 * rows), jnp.float32),
+            jax.ShapeDtypeStruct((slots, width), jnp.bfloat16),
+        ),
+        in_specs=[smem, vmem, hbm, vmem, hbm, vmem, vmem, vmem, vmem, smem],
+        out_specs=(vmem, vmem, vmem),
         scratch_shapes=[
             pltpu.VMEM((4, slots, width), jnp.bfloat16),
             pltpu.VMEM((4 * slots + PAD, width), jnp.float32),
@@ -341,12 +441,18 @@
             pltpu.VMEM((CHUNKS, 2, block // 2, columns), jnp.bfloat16),
             pltpu.VMEM((CHUNKS, 2, block, columns), jnp.bfloat16),
             pltpu.VMEM((CHUNKS, 2, block, columns), jnp.bfloat16),
+            pltpu.VMEM((4, hold, 2 * width), jnp.bfloat16),
+            pltpu.VMEM((4, 1, hold), jnp.int32),
+            pltpu.VMEM((4, 8, 4 * rows), jnp.float32),
             pltpu.SemaphoreType.DMA((2,)),
             pltpu.SemaphoreType.DMA((4,)),
             pltpu.SemaphoreType.DMA((4,)),
             pltpu.SemaphoreType.DMA((CHUNKS,)),
             pltpu.SemaphoreType.DMA((CHUNKS,)),
             *pairs,
+            pltpu.SemaphoreType.DMA((4,)),
+            pltpu.SemaphoreType.DMA((4,)),
+            *[pltpu.SemaphoreType.DMA((3,))] * 4,
         ],
         compiler_params=pltpu.CompilerParams(
             collective_id=1, has_side_effects=True, vmem_limit_bytes=56 << 20
@@ -357,7 +463,18 @@
             transcendentals=0,
         ),
         name="top_network",
-    )(indices, cache_table, w_first, b_first[None], w_second, b_second[None])
+    )(
+        indices,
+        cache_table,
+        w_first,
+        b_first[None],
+        w_second,
+        b_second[None],
+        jnp.broadcast_to(w_out[None], (16, columns)),
+        miss_rows,
+        miss_slots,
+        counts,
+    )
 
 
 def body(
@@ -390,26 +507,21 @@
     indices = jnp.where(used, by_lookup, narrow_count * slot_count)
     indices = indices.transpose(1, 0, 2).reshape(wide_count * bag_size * rows)
 
-    top_hidden = top_network(
-        indices, cache_table, w_first, b_first, w_second, b_second, bag_size, wide_count
+    top_hidden, logits, cache_next = top_network(
+        indices,
+        cache_table,
+        w_first,
+        b_first,
+        w_second,
+        b_second,
+        w_out,
+        miss_rows[0],
+        miss_slots,
+        holder_counts[0],
+        bag_size,
+        wide_count,
     )
-    logit_term = jnp.dot(top_hidden, w_out, preferred_element_type=jnp.float32)
-    logits = jnp.sum(copy_for_each(logit_term, "narrow"), axis=0)
-
-    total = jnp.sum(holder_counts[0])
-    hold_rows = miss_slots.shape[1]
-    live = jnp.arange(hold_rows, dtype=jnp.int32) < total
-    held_slots = jnp.where(live, miss_slots[0], -1)
-    all_slots = copy_for_each(held_slots, "narrow").reshape(narrow_count * hold_rows)
-    all_rows = copy_for_each(miss_rows[0], "narrow").reshape(narrow_count * hold_rows, width)
-    targets = all_slots - position * slot_count
-    placing = targets[None, :] == jnp.arange(slot_count, dtype=jnp.int32)[:, None]
-    placed = jnp.dot(
-        placing.astype(jnp.bfloat16), all_rows, preferred_element_type=jnp.float32
-    )
-    struck = jnp.any(placing, axis=1)
-    cache_next = jnp.where(struck[:, None], placed.astype(jnp.bfloat16), cache_table)[None]
-    return (top_hidden, logits, cache_next)
+    return (top_hidden, logits[0], cache_next[None])
 
 
 def solution(mesh):

time: 191 us -> 161 us (0.84)
  waiting for transfers between devices: 9.82 us -> 0 us
  matrix products: 8.44 us -> 0 us
  starting transfers between devices: 7.76 us -> 0 us
  blocking collectives: 7.71 us -> 0 us
  other arithmetic: 7.04 us -> 0.88 us
  Pallas kernels: 144 us -> 149 us
  local copies, waits for them, and re-layouts: 5.68 us -> 9.72 us
    all_to_all x2 -> x0, waiting for transfers between devices: 9.82 us -> none  [copy_for_each(): lax.all_to_all(jnp.broadcast_to(x[None], (length, *x.shape)), axis, 0, 0,...]
    dot_general x2 -> x0, matrix products: 8.44 us -> none  [the longest x1 6.85 us: body(): jnp.dot(placing.astype(jnp.bfloat16), all_rows, preferred_element_type=jn...]
    all_to_all x2 -> x0, starting transfers between devices: 7.76 us -> none  [copy_for_each(): lax.all_to_all(jnp.broadcast_to(x[None], (length, *x.shape)), axis, 0, 0,...]
    all_to_all x1 -> x0, blocking collectives: 7.71 us -> none  [copy_for_each(): lax.all_to_all(jnp.broadcast_to(x[None], (length, *x.shape)), axis, 0, 0,...]
    pallas_call x1, Pallas kernels: 144 us -> 149 us  [top_network(): pl.pallas_call(functools.partial(top_kernel, bag_size, wide_count), out_s...]
    unnamed x14 -> x5, local copies, waits for them, and re-layouts: 1.69 us -> 6.19 us
    reduce_or x1 -> x0, other arithmetic: 4.26 us -> none  [body(): struck = jnp.any(placing, axis=1)]
  transfers between devices with their start and end apart: 2 -> 0, of which waited for: 2 -> 0; matrix products, arithmetic and copies ran while one was open for 3% -> 0% of each run, Pallas kernels for 0% -> 0%
where the time goes in v3:
time: 161 us; the launch traced here: 160 us
  Pallas kernels  149 us (93%)
  local copies, waits for them, and re-layouts  9.72 us (6%)
    pallas_call x1, Pallas kernels, top_network(): pl.pallas_call(functools.partial(top_kernel, bag_size, wide_count), out_s...  149 us
    unnamed x5, local copies, waits for them, and re-layouts  6.19 us

profile of v3, /device:TPU:0, one launch (start us, length us, event | category | flops | bytes accessed | tf_op | source)
XLA Modules:
  0.0 160.4 jit_solution(8142529802912095536)
XLA Ops:
  0.6 0.0 copy-start
  0.6 0.8 copy-done
  1.5 1.3 broadcast_in_dim.24.w_out_ref
  2.8 1.9 %reshape.15 = s32[16,32,4,128]{3,2,1,0:T(4,128)S(1)} reshape(s32[16,16384]{1,0:T(8,128)} %bitcast.20) | data formatting | bytes 2097152 | tf_op jit(solution)/shard_map/reshape | solution.py:502
  4.7 0.3 constant_dynamic-slice_fusion
  5.0 0.9 fusion
  5.9 149.1 %top_network.1 = (bf16[512,1024]{1,0:T(8,128)(2,1)}, f32[1,512]{1,0:T(1,128)}, bf16[2048,128]{1,0:T(8,128)(2,1)}) custom-call(s32[65536]{0:T(1024)} %bitcast.22, bf16[2048,128]{1,0:T(8,128)(2,1)} %bitcast.25, bf16[4096,1024]{1,0:T(8,128)(2,1)} %w_first_hbm.1, f32[1,1024]{1,0:T(1,128)} %bitcast.27, bf16[1024,4096]{1,0:T(8,128)(2,1)} %w_second_hbm.1, ...), custom_call_target="tpu_custom_call" | custom-call | flops 8589934592 | bytes 16777216 | tf_op jit(solution)/shard_map/top_network/pallas_call | solution.py:419
  155.0 2.3 %copy.22 = bf16[512,1024]{1,0:T(8,128)(2,1)} copy(bf16[512,1024]{1,0:T(8,128)(2,1)} %get-tuple-element.12) | data formatting | bytes 2097152
  157.3 1.2 copy.23
  158.5 1.9 %copy.24 = bf16[1,2048,128]{2,1,0:T(8,128)(2,1)} copy(bf16[1,2048,128]{2,1,0:T(8,128)(2,1)} %bitcast.21) | data formatting | bytes 1048576
  (1 shorter events, 0.0 us)
Async XLA Ops:
  0.6 0.8 copy-start

commit v4 on v3

v4 whole, which is shorter than its diff:
```python
import jax
import jax.numpy as jnp
from jax import lax
from jax.experimental import pallas as pl
from jax.experimental.pallas import tpu as pltpu
from jax.sharding import PartitionSpec as P

COUNTS = (32, 32, 32, 32)
STEPS = 4
PAD = 16
UNROLL = 16
TILE = 256
MESH = pl.DeviceIdType.MESH


def top_kernel(
    lookups_hbm,
    lengths_hbm,
    cache_ref,
    w_first_hbm,
    b_first_ref,
    w_second_hbm,
    b_second_ref,
    w_out_ref,
    miss_rows_ref,
    miss_slots_ref,
    counts_ref,
    top_ref,
    logits_ref,
    cache_next_ref,
    lookups,
    lengths,
    index_ref,
    table,
    wide_table,
    pooled,
    sums,
    features,
    hidden,
    w_first,
    w_second,
    own_part,
    right_part,
    left_part,
    far_out,
    far_in,
    near_out,
    near_in,
    held_rows,
    held_slots,
    logit_parts,
    index_sem,
    weight_sem,
    table_send,
    table_recv,
    exchange_send,
    exchange_recv,
    gather_send,
    gather_recv,
    pass_send,
    pass_recv,
    far_send,
    far_recv,
    near_send,
    near_recv,
    rows_send,
    rows_recv,
    slots_send,
    slots_recv,
    logit_send,
    logit_recv,
):
    me = lax.axis_index("wide")
    place = lax.axis_index("narrow")
    right, left = lax.rem(place + 1, 4), lax.rem(place + 3, 4)
    slots, width = cache_ref.shape
    wide_count, rows, _ = pooled.shape
    bag_size = lookups.shape[1]
    owner_rows = 4 * rows
    chunks = len(COUNTS)
    starts = tuple(sum(COUNTS[:chunk]) for chunk in range(chunks))
    fan_in, columns = w_first.shape
    sides = ((0, right), (1, left))
    opposite = lax.rem(place + 2, 4)
    everyone = ((0, right), (1, left), (2, opposite))

    def own_span(owner):
        return pl.ds(pl.multiple_of((owner * 4 + place) * rows, rows), rows)

    def fetch(owner, _):
        pltpu.make_async_copy(lookups_hbm.at[:, own_span(owner)], lookups.at[owner], index_sem.at[0]).start()
        return 0

    lax.fori_loop(0, wide_count, fetch, 0)
    lengths_copy = pltpu.make_async_copy(lengths_hbm, lengths, index_sem.at[1])
    lengths_copy.start()
    first_copy = pltpu.make_async_copy(w_first_hbm, w_first, weight_sem.at[0])
    second_copy = pltpu.make_async_copy(w_second_hbm, w_second, weight_sem.at[1])
    first_copy.start()
    second_copy.start()

    barrier = pltpu.get_barrier_semaphore()

    def greet(i, _):
        pl.semaphore_signal(
            barrier, inc=1, device_id={"wide": lax.rem(me + i, wide_count)}, device_id_type=MESH
        )
        return 0

    lax.fori_loop(1, wide_count, greet, 0)
    for _, other in everyone:
        pl.semaphore_signal(barrier, inc=1, device_id={"narrow": other}, device_id_type=MESH)

    hold = miss_rows_ref.shape[0]
    total = counts_ref[0] + counts_ref[1] + counts_ref[2] + counts_ref[3]
    position = lax.broadcasted_iota(jnp.int32, (1, hold), 1)
    held_slots[place] = jnp.where(position < total, miss_slots_ref[...], -1)
    held_rows[:, :, width:] = jnp.ones((4, hold, width), jnp.bfloat16)
    held_rows[place, :, :width] = miss_rows_ref[...]

    pl.semaphore_wait(barrier, wide_count + 2)

    def to_side(source, target, send, recv, other):
        return pltpu.make_async_remote_copy(
            src_ref=source,
            dst_ref=target,
            send_sem=send,
            recv_sem=recv,
            device_id={"narrow": other},
            device_id_type=MESH,
        )

    half = slots // 2
    near_tables = []
    for late in range(2):
        for k, other in sides:
            span = pl.ds((late ^ k) * half, half)
            near_tables.append(
                to_side(
                    cache_ref.at[span],
                    table.at[place, span],
                    table_send.at[2 * late + k],
                    table_recv.at[2 * late + k],
                    other,
                )
            )
    for copy in near_tables:
        copy.start()
    wide_table[pl.ds(pl.multiple_of(place * slots, slots), slots), :] = cache_ref[...].astype(jnp.float32)
    wide_table[4 * slots :, :] = jnp.zeros((PAD, width), jnp.float32)

    pltpu.make_async_copy(lookups, lookups, index_sem.at[0]).wait()
    lengths_copy.wait()

    def mask(owner, _):
        number = lax.broadcasted_iota(jnp.int32, (bag_size, rows), 0)
        lookups[owner] = jnp.where(number < lengths[:, own_span(owner)], lookups[owner], 4 * slots)
        return 0

    lax.fori_loop(0, wide_count, mask, 0)
    index_copy = pltpu.make_async_copy(lookups, index_ref, index_sem.at[2])
    index_copy.start()
    far_tables = []
    for k, other, source in ((0, right, left), (1, left, right)):
        near_tables[k].wait_recv()
        part = table.at[source, pl.ds(k * half, half)]
        copy = to_side(part, part, table_send.at[4 + k], table_recv.at[4 + k], other)
        copy.start()
        far_tables.append(copy)

    def widen(source):
        wide_table[pl.ds(pl.multiple_of(source * slots, slots), slots), :] = table[source].astype(jnp.float32)

    for copy in near_tables[2:]:
        copy.wait_recv()
    widen(left)
    widen(right)
    for copy in far_tables:
        copy.wait_recv()
    widen(opposite)
    index_copy.wait()

    slot_copies = [
        to_side(held_slots.at[place], held_slots.at[place], slots_send.at[k], slots_recv.at[k], other)
        for k, other in everyone
    ]
    own_held = held_rows.at[place, :, pl.ds(0, width)]
    near_held = [
        to_side(own_held, own_held, rows_send.at[k], rows_recv.at[k], other) for k, other in sides
    ]
    for copy in slot_copies + near_held:
        copy.start()
    far_held = []
    for k, other, source in ((0, right, left), (1, left, right)):
        part = held_rows.at[source, pl.ds(k * (hold // 2), hold // 2), pl.ds(0, width)]
        far_held.append(to_side(part, part, rows_send.at[2 + k], rows_recv.at[2 + k], other))

    def pass_held():
        for near, far in zip(near_held, far_held):
            near.wait_recv()
            far.start()

    def held_arrived():
        for copy in slot_copies + far_held:
            copy.wait_recv()

    def refill(low, high):
        def step(t, _):
            span = pl.ds(pl.multiple_of(t * TILE, TILE), TILE)
            slot = place * slots + t * TILE + lax.broadcasted_iota(jnp.int32, (TILE, hold), 0)
            placed = jnp.zeros((TILE, 2 * width), jnp.float32)
            for q in range(4):
                chosen = jnp.where(held_slots[q] == slot, 1.0, 0.0).astype(jnp.bfloat16)
                placed += jnp.dot(chosen, held_rows[q], preferred_element_type=jnp.float32)
            cache_next_ref[span, :] = jnp.where(
                placed[:, width:] > 0.5, placed[:, :width].astype(jnp.bfloat16), cache_ref[span, :]
            )
            return 0

        lax.fori_loop(low, high, step, 0)

    def pool(chunk, low, high):
        count, start = COUNTS[chunk], starts[chunk]

        def owner_step(i, _):
            owner = lax.rem(me + i, wide_count)
            for row in range(0, count, UNROLL):
                for u in range(row, row + UNROLL):
                    terms = [
                        wide_table[pl.ds(index_ref[owner, l, start + u], 1), :] for l in range(bag_size)
                    ]
                    while len(terms) > 1:
                        terms = [terms[k] + terms[k + 1] for k in range(0, len(terms), 2)]
                    sums[pl.ds(u, 1), :] = terms[0]
            source = pooled.at[owner, pl.ds(start, count)]
            source[...] = sums[:count, :].astype(jnp.bfloat16)
            target = features.at[
                pl.ds(pl.multiple_of(4 * start + place * count, 16), count),
                pl.ds(pl.multiple_of(me * width, width), width),
            ]

            @pl.when(i == 0)
            def _():
                pltpu.make_async_copy(source, target, exchange_recv.at[chunk]).start()

            @pl.when(i > 0)
            def _():
                pltpu.make_async_remote_copy(
                    src_ref=source,
                    dst_ref=target,
                    send_sem=exchange_send.at[chunk],
                    recv_sem=exchange_recv.at[chunk],
                    device_id={"wide": owner},
                    device_id_type=MESH,
                ).start()

            return 0

        lax.fori_loop(low, high, owner_step, 0)

    def own_rows(chunk, source):
        return pl.ds(pl.multiple_of(4 * starts[chunk] + source * COUNTS[chunk], 16), COUNTS[chunk])

    def near_copies(chunk):
        part = features.at[own_rows(chunk, place)]
        return [
            to_side(part, part, gather_send.at[chunk, k], gather_recv.at[chunk, k], other)
            for k, other in sides
        ]

    def pass_copies(chunk):
        found = []
        for k, other, source in ((0, right, left), (1, left, right)):
            view = features.at[own_rows(chunk, source), pl.ds(k * (fan_in // 2), fan_in // 2)]
            found.append(to_side(view, view, pass_send.at[chunk, k], pass_recv.at[chunk, k], other))
        return found

    def far_copies(chunk):
        span = pl.ds(2 * starts[chunk], 2 * COUNTS[chunk])
        return [
            to_side(far_out.at[k, span], far_in.at[k, span], far_send.at[chunk, k], far_recv.at[chunk, k], other)
            for k, other in sides
        ]

    def near_sums(chunk):
        span = pl.ds(4 * starts[chunk], 4 * COUNTS[chunk])
        return [
            to_side(near_out.at[k, span], near_in.at[k, span], near_send.at[chunk, k], near_recv.at[chunk, k], other)
            for k, other in sides
        ]

    def exchanged(chunk):
        whole = features.at[own_rows(chunk, place)]
        pltpu.make_async_copy(whole, whole, exchange_recv.at[chunk]).wait()
        for copy in near_copies(chunk):
            copy.start()

    def pass_on(chunk):
        for near, on in zip(near_copies(chunk), pass_copies(chunk)):
            near.wait_recv()
            on.start()

    def layers(chunk):
        block, middle = 4 * COUNTS[chunk], 2 * COUNTS[chunk]
        begin = 4 * starts[chunk]
        for copy in pass_copies(chunk):
            copy.wait_recv()
        if chunk == 0:
            first_copy.wait()
            second_copy.wait()

        def first(t, _):
            span = pl.ds(pl.multiple_of(t * TILE, TILE), TILE)
            terms = jnp.dot(features[pl.ds(begin, block), :], w_first[:, span], preferred_element_type=jnp.float32)
            hidden[:block, span] = jnp.maximum(terms + b_first_ref[:, span], 0.0).astype(jnp.bfloat16)
            return 0

        lax.fori_loop(0, columns // TILE, first, 0, unroll=True)

        def second(ahead, keep):
            target = lax.rem(place + ahead, 4)

            def step(t, _):
                span = pl.ds(pl.multiple_of(t * TILE, TILE), TILE)
                from_ = pl.ds(pl.multiple_of(target * columns + t * TILE, TILE), TILE)
                keep(span, jnp.dot(hidden[:block, :], w_second[:, from_], preferred_element_type=jnp.float32))
                return 0

            lax.fori_loop(0, columns // TILE, step, 0, unroll=True)

        def keep_far(span, terms):
            for k in range(2):
                half_rows = terms[k * middle : (k + 1) * middle]
                far_out[k, pl.ds(2 * starts[chunk], middle), span] = half_rows.astype(jnp.bfloat16)

        second(2, keep_far)
        for copy in far_copies(chunk):
            copy.start()

        def keep_right(span, terms):
            right_part[:block, span] = terms

        def keep_left(span, terms):
            left_part[:block, span] = terms

        def keep_own(span, terms):
            own_part[pl.ds(begin, block), span] = terms

        second(1, keep_right)
        second(3, keep_left)
        second(0, keep_own)

    def join(chunk):
        middle, begin = 2 * COUNTS[chunk], 4 * starts[chunk]
        parts = (right_part, left_part)
        for k, copy in enumerate(far_copies(chunk)):
            copy.wait_recv()
            summed, alone = k * middle, (1 - k) * middle
            came = far_in[k, pl.ds(2 * starts[chunk], middle), :].astype(jnp.float32)
            near_out[k, pl.ds(begin + summed, middle), :] = (
                parts[k][pl.ds(summed, middle), :] + came
            ).astype(jnp.bfloat16)
            near_out[k, pl.ds(begin + alone, middle), :] = parts[k][pl.ds(alone, middle), :].astype(jnp.bfloat16)
        for copy in near_sums(chunk):
            copy.start()

    def finish(chunk):
        for copy in near_sums(chunk):
            copy.wait_recv()
        count = COUNTS[chunk]
        for q in range(4):
            span = pl.ds(4 * starts[chunk] + q * count, count)
            terms = own_part[span, :] + near_in[0, span, :].astype(jnp.float32) + near_in[1, span, :].astype(jnp.float32)
            top_ref[pl.ds(q * rows + starts[chunk], count), :] = jnp.maximum(
                terms + b_second_ref[...], 0.0
            ).astype(jnp.bfloat16)

    part = wide_count // STEPS
    blocks = slots // TILE
    for chunk in range(chunks):
        for step in range(STEPS):
            pool(chunk, step * part, (step + 1) * part)
            if chunk == 0 and step == 1:
                pass_held()
            if step == 0 and chunk >= 1:
                exchanged(chunk - 1)
            if step == 1 and chunk >= 2:
                layers(chunk - 2)
            if step == 2 and chunk >= 1:
                pass_on(chunk - 1)
            if step == 3 and chunk >= 2:
                join(chunk - 2)
            if step == 1 and chunk >= 3:
                finish(chunk - 3)
    last = chunks - 1
    exchanged(last)
    layers(last - 1)
    held_arrived()
    finish(last - 2)
    pass_on(last)
    refill(0, blocks // 2)
    join(last - 1)
    layers(last)
    refill(blocks // 2, blocks)
    join(last)
    finish(last - 1)
    finish(last)

    logit_parts[place] = lax.dot_general(
        jnp.broadcast_to(w_out_ref[...], (8, columns)).astype(jnp.bfloat16),
        top_ref[...],
        (((1,), (1,)), ((), ())),
        preferred_element_type=jnp.float32,
    )
    logit_copies = [
        to_side(logit_parts.at[place], logit_parts.at[place], logit_send.at[k], logit_recv.at[k], other)
        for k, other in everyone
    ]
    for copy in logit_copies:
        copy.start()
    for chunk in range(chunks):
        sent = pooled.at[pl.ds(0, wide_count - 1), pl.ds(0, COUNTS[chunk])]
        pltpu.make_async_copy(sent, sent, exchange_send.at[chunk]).wait()
        for copies in (near_copies, pass_copies, far_copies, near_sums):
            for copy in copies(chunk):
                copy.wait_send()
    for copy in near_tables + far_tables + slot_copies + near_held + far_held:
        copy.wait_send()
    for copy in logit_copies:
        copy.wait_recv()
    logits_ref[...] = (
        logit_parts[0][:1] + logit_parts[1][:1] + (logit_parts[2][:1] + logit_parts[3][:1])
    )
    for copy in logit_copies:
        copy.wait_send()


def top_network(
    lookups,
    lengths,
    cache_table,
    w_first,
    b_first,
    w_second,
    b_second,
    w_out,
    miss_rows,
    miss_slots,
    counts,
    wide_count,
):
    slots, width = cache_table.shape
    bag_size, batch_rows = lookups.shape
    rows = batch_rows // (4 * wide_count)
    chunks = len(COUNTS)
    block = 4 * max(COUNTS)
    fan_in, columns = w_first.shape
    vmem = pl.BlockSpec(memory_space=pltpu.VMEM)
    hbm = pl.BlockSpec(memory_space=pl.ANY)
    smem = pl.BlockSpec(memory_space=pltpu.SMEM)
    hold = miss_rows.shape[0]
    pairs = [pltpu.SemaphoreType.DMA((chunks, 2))] * 8
    return pl.pallas_call(
        top_kernel,
        out_shape=(
            jax.ShapeDtypeStruct((4 * rows, columns), jnp.bfloat16),
            jax.ShapeDtypeStruct((1, 4 * rows), jnp.float32),
            jax.ShapeDtypeStruct((slots, width), jnp.bfloat16),
        ),
        in_specs=[hbm, hbm, vmem, hbm, vmem, hbm, vmem, vmem, vmem, vmem, smem],
        out_specs=(vmem, vmem, vmem),
        scratch_shapes=[
            pltpu.VMEM((wide_count, bag_size, rows), jnp.int32),
            pltpu.VMEM((1, batch_rows), jnp.int32),
            pltpu.SMEM((wide_count, bag_size, rows), jnp.int32),
            pltpu.VMEM((4, slots, width), jnp.bfloat16),
            pltpu.VMEM((4 * slots + PAD, width), jnp.float32),
            pltpu.VMEM((wide_count, rows, width), jnp.bfloat16),
            pltpu.VMEM((max(COUNTS), width), jnp.float32),
            pltpu.VMEM((4 * rows, fan_in), jnp.bfloat16),
            pltpu.VMEM((block, columns), jnp.bfloat16),
            pltpu.VMEM((fan_in, columns), jnp.bfloat16),
            pltpu.VMEM((columns, fan_in), jnp.bfloat16),
            pltpu.VMEM((4 * rows, columns), jnp.float32),
            pltpu.VMEM((block, columns), jnp.float32),
            pltpu.VMEM((block, columns), jnp.float32),
            pltpu.VMEM((2, 2 * rows, columns), jnp.bfloat16),
            pltpu.VMEM((2, 2 * rows, columns), jnp.bfloat16),
            pltpu.VMEM((2, 4 * rows, columns), jnp.bfloat16),
            pltpu.VMEM((2, 4 * rows, columns), jnp.bfloat16),
            pltpu.VMEM((4, hold, 2 * width), jnp.bfloat16),
            pltpu.VMEM((4, 1, hold), jnp.int32),
            pltpu.VMEM((4, 8, 4 * rows), jnp.float32),
            pltpu.SemaphoreType.DMA((3,)),
            pltpu.SemaphoreType.DMA((2,)),
            pltpu.SemaphoreType.DMA((6,)),
            pltpu.SemaphoreType.DMA((6,)),
            pltpu.SemaphoreType.DMA((chunks,)),
            pltpu.SemaphoreType.DMA((chunks,)),
            *pairs,
            pltpu.SemaphoreType.DMA((4,)),
            pltpu.SemaphoreType.DMA((4,)),
            *[pltpu.SemaphoreType.DMA((3,))] * 4,
        ],
        compiler_params=pltpu.CompilerParams(
            collective_id=1, has_side_effects=True, vmem_limit_bytes=56 << 20
        ),
        cost_estimate=pl.CostEstimate(
            flops=4 * 4 * rows * fan_in * columns,
            bytes_accessed=2 * 2 * fan_in * columns,
            transcendentals=0,
        ),
        name="top_network",
    )(
        lookups,
        lengths,
        cache_table,
        w_first,
        b_first[None],
        w_second,
        b_second[None],
        w_out.astype(jnp.float32)[None],
        miss_rows,
        miss_slots,
        counts,
    )


def copy_kernel(*refs):
    count = len(refs) // 2
    for k in range(count):
        refs[count + k][...] = refs[k][...]


def copied(*arrays):
    vmem = pl.BlockSpec(memory_space=pltpu.VMEM)
    return pl.pallas_call(
        copy_kernel,
        out_shape=tuple(jax.ShapeDtypeStruct(a.shape, a.dtype) for a in arrays),
        in_specs=[vmem] * len(arrays),
        out_specs=(vmem,) * len(arrays),
        name="copied",
    )(*arrays)


def body(
    cache,
    lookup_slots,
    bag_lengths,
    miss_rows,
    miss_slots,
    holder_counts,
    w_first,
    b_first,
    w_second,
    b_second,
    w_out,
):
    top_hidden, logits, cache_next = copied(
        *top_network(
            lookup_slots[0].T,
            bag_lengths,
            cache[0],
            w_first,
            b_first,
            w_second,
            b_second,
            w_out,
            miss_rows[0],
            miss_slots,
            holder_counts[0],
            lax.axis_size("wide"),
        )
    )
    return (top_hidden, logits[0], cache_next[None])


def solution(mesh):
    return jax.shard_map(
        body,
        mesh=mesh,
        in_specs=(
            P("wide", "narrow", None),
            P("wide", None, None),
            P("wide", None),
            P("wide", "narrow", None),
            P("wide", "narrow"),
            P("wide", "narrow"),
            P(None, "narrow"),
            P("narrow"),
            P("narrow", None),
            P("narrow"),
            P("narrow"),
        ),
        out_specs=(P("wide", "narrow"), P("wide"), P("wide", "narrow", None)),
        check_vma=False,
    )
```

time: 161 us -> 145 us (0.901)
  local copies, waits for them, and re-layouts: 9.72 us -> 0 us
  Pallas kernels: 149 us -> 142 us
    pallas_call x1 -> x2, Pallas kernels: 149 us -> 142 us  [the longest x1 140 us: top_network(): pl.pallas_call(top_kernel, out_shape=(jax.ShapeDtypeStruct((4 * rows, col...]
    unnamed x5 -> x0, local copies, waits for them, and re-layouts: 6.19 us -> none
    reshape x1 -> x0, local copies, waits for them, and re-layouts: 1.93 us -> none  [body(): lookup_slots[0].T.reshape(bag_size, wide_count, narrow_count, rows)]
where the time goes in v4:
time: 145 us; the launch traced here: 144 us
  Pallas kernels  142 us (98%)
    pallas_call x1, Pallas kernels, top_network(): pl.pallas_call(top_kernel, out_shape=(jax.ShapeDtypeStruct((4 * rows, col...  140 us

profile of v4, /device:TPU:0, one launch (start us, length us, event | category | flops | bytes accessed | tf_op | source)
XLA Modules:
  0.0 144.4 jit_solution(6974240691984290513)
XLA Ops:
  0.6 1.3 broadcast_in_dim.19
  1.9 139.9 %top_network.1 = (bf16[512,1024]{1,0:T(8,128)(2,1)}, f32[1,512]{1,0:T(1,128)}, bf16[2048,128]{1,0:T(8,128)(2,1)}) custom-call(s32[16,16384]{1,0:T(8,128)} %bitcast.12, s32[1,16384]{1,0:T(1,128)} %lengths_hbm.1, bf16[2048,128]{1,0:T(8,128)(2,1)} %bitcast.13, bf16[4096,1024]{1,0:T(8,128)(2,1)} %w_first_hbm.1, f32[1,1024]{1,0:T(1,128)} %bitcast.16, ...), custom_call_target="tpu_custom_call" | custom-call | flops 8589934592 | bytes 16777216 | tf_op jit(solution)/shard_map/top_network/pallas_call | solution.py:463
  141.8 2.6 %copied.1 = (bf16[512,1024]{1,0:T(8,128)(2,1)}, f32[1,512]{1,0:T(1,128)}, bf16[2048,128]{1,0:T(8,128)(2,1)}) custom-call(bf16[512,1024]{1,0:T(8,128)(2,1)} %get-tuple-element.9.refs_0_, f32[1,512]{1,0:T(1,128)} %get-tuple-element.10.refs_1_, bf16[2048,128]{1,0:T(8,128)(2,1)} %get-tuple-element.11.refs_2_), custom_call_target="tpu_custom_call" | custom-call | tf_op jit(solution)/shard_map/copied/pallas_call | solution.py:537

commit v5 on v4

--- a/solution.py
+++ b/solution.py
@@ -1,3 +1,5 @@
+import functools
+
 import jax
 import jax.numpy as jnp
 from jax import lax
@@ -63,6 +65,10 @@
     far_recv,
     near_send,
     near_recv,
+    late_send,
+    late_recv,
+    lone_send,
+    lone_recv,
     rows_send,
     rows_recv,
     slots_send,
@@ -261,12 +267,19 @@
     def own_rows(chunk, source):
         return pl.ds(pl.multiple_of(4 * starts[chunk] + source * COUNTS[chunk], 16), COUNTS[chunk])
 
+    def side_halves(chunk, late, send, recv):
+        found = []
+        for k, other in sides:
+            columns_half = pl.ds((late ^ k) * (fan_in // 2), fan_in // 2)
+            part = features.at[own_rows(chunk, place), columns_half]
+            found.append(to_side(part, part, send.at[chunk, k], recv.at[chunk, k], other))
+        return found
+
     def near_copies(chunk):
-        part = features.at[own_rows(chunk, place)]
-        return [
-            to_side(part, part, gather_send.at[chunk, k], gather_recv.at[chunk, k], other)
-            for k, other in sides
-        ]
+        return side_halves(chunk, 0, gather_send, gather_recv)
+
+    def late_copies(chunk):
+        return side_halves(chunk, 1, late_send, late_recv)
 
     def pass_copies(chunk):
         found = []
@@ -282,17 +295,26 @@
             for k, other in sides
         ]
 
+    def sum_halves(chunk, lone, send, recv):
+        middle = 2 * COUNTS[chunk]
+        found = []
+        for k, other in sides:
+            span = pl.ds(4 * starts[chunk] + (lone ^ k) * middle, middle)
+            found.append(
+                to_side(near_out.at[k, span], near_in.at[k, span], send.at[chunk, k], recv.at[chunk, k], other)
+            )
+        return found
+
     def near_sums(chunk):
-        span = pl.ds(4 * starts[chunk], 4 * COUNTS[chunk])
-        return [
-            to_side(near_out.at[k, span], near_in.at[k, span], near_send.at[chunk, k], near_recv.at[chunk, k], other)
-            for k, other in sides
-        ]
+        return sum_halves(chunk, 0, near_send, near_recv)
+
+    def lone_sums(chunk):
+        return sum_halves(chunk, 1, lone_send, lone_recv)
 
     def exchanged(chunk):
         whole = features.at[own_rows(chunk, place)]
         pltpu.make_async_copy(whole, whole, exchange_recv.at[chunk]).wait()
-        for copy in near_copies(chunk):
+        for copy in near_copies(chunk) + late_copies(chunk):
             copy.start()
 
     def pass_on(chunk):
@@ -303,7 +325,7 @@
     def layers(chunk):
         block, middle = 4 * COUNTS[chunk], 2 * COUNTS[chunk]
         begin = 4 * starts[chunk]
-        for copy in pass_copies(chunk):
+        for copy in late_copies(chunk) + pass_copies(chunk):
             copy.wait_recv()
         if chunk == 0:
             first_copy.wait()
@@ -348,6 +370,11 @@
 
         second(1, keep_right)
         second(3, keep_left)
+        for k, part in enumerate((right_part, left_part)):
+            lone = (1 - k) * middle
+            near_out[k, pl.ds(begin + lone, middle), :] = part[pl.ds(lone, middle), :].astype(jnp.bfloat16)
+        for copy in lone_sums(chunk):
+            copy.start()
         second(0, keep_own)
 
     def join(chunk):
@@ -355,17 +382,16 @@
         parts = (right_part, left_part)
         for k, copy in enumerate(far_copies(chunk)):
             copy.wait_recv()
-            summed, alone = k * middle, (1 - k) * middle
+            summed = k * middle
             came = far_in[k, pl.ds(2 * starts[chunk], middle), :].astype(jnp.float32)
             near_out[k, pl.ds(begin + summed, middle), :] = (
                 parts[k][pl.ds(summed, middle), :] + came
             ).astype(jnp.bfloat16)
-            near_out[k, pl.ds(begin + alone, middle), :] = parts[k][pl.ds(alone, middle), :].astype(jnp.bfloat16)
         for copy in near_sums(chunk):
             copy.start()
 
     def finish(chunk):
-        for copy in near_sums(chunk):
+        for copy in lone_sums(chunk) + near_sums(chunk):
             copy.wait_recv()
         count = COUNTS[chunk]
         for q in range(4):
@@ -395,11 +421,11 @@
     last = chunks - 1
     exchanged(last)
     layers(last - 1)
-    held_arrived()
     finish(last - 2)
     pass_on(last)
+    join(last - 1)
+    held_arrived()
     refill(0, blocks // 2)
-    join(last - 1)
     layers(last)
     refill(blocks // 2, blocks)
     join(last)
@@ -407,7 +433,7 @@
     finish(last)
 
     logit_parts[place] = lax.dot_general(
-        jnp.broadcast_to(w_out_ref[...], (8, columns)).astype(jnp.bfloat16),
+        jnp.broadcast_to(w_out_ref[...].astype(jnp.float32), (8, columns)).astype(jnp.bfloat16),
         top_ref[...],
         (((1,), (1,)), ((), ())),
         preferred_element_type=jnp.float32,
@@ -421,7 +447,7 @@
     for chunk in range(chunks):
         sent = pooled.at[pl.ds(0, wide_count - 1), pl.ds(0, COUNTS[chunk])]
         pltpu.make_async_copy(sent, sent, exchange_send.at[chunk]).wait()
-        for copies in (near_copies, pass_copies, far_copies, near_sums):
+        for copies in (near_copies, late_copies, pass_copies, far_copies, lone_sums, near_sums):
             for copy in copies(chunk):
                 copy.wait_send()
     for copy in near_tables + far_tables + slot_copies + near_held + far_held:
@@ -459,7 +485,7 @@
     hbm = pl.BlockSpec(memory_space=pl.ANY)
     smem = pl.BlockSpec(memory_space=pltpu.SMEM)
     hold = miss_rows.shape[0]
-    pairs = [pltpu.SemaphoreType.DMA((chunks, 2))] * 8
+    pairs = [pltpu.SemaphoreType.DMA((chunks, 2))] * 12
     return pl.pallas_call(
         top_kernel,
         out_shape=(
@@ -519,26 +545,39 @@
         b_first[None],
         w_second,
         b_second[None],
-        w_out.astype(jnp.float32)[None],
+        w_out[None],
         miss_rows,
         miss_slots,
         counts,
     )
 
 
-def copy_kernel(*refs):
-    count = len(refs) // 2
-    for k in range(count):
-        refs[count + k][...] = refs[k][...]
+def copy_kernel(count, *refs):
+    sources, targets, held = refs[:count], refs[count : 2 * count], refs[2 * count : 3 * count]
+    sems = refs[3 * count]
+    ins = [pltpu.make_async_copy(sources[k], held[k], sems.at[0, k]) for k in range(count)]
+    outs = [pltpu.make_async_copy(held[k], targets[k], sems.at[1, k]) for k in range(count)]
+    for copy in ins:
+        copy.start()
+    for arrived, leave in zip(ins, outs):
+        arrived.wait()
+        leave.start()
+    for copy in outs:
+        copy.wait()
 
 
 def copied(*arrays):
-    vmem = pl.BlockSpec(memory_space=pltpu.VMEM)
+    hbm = pl.BlockSpec(memory_space=pl.ANY)
+    count = len(arrays)
     return pl.pallas_call(
-        copy_kernel,
+        functools.partial(copy_kernel, count),
         out_shape=tuple(jax.ShapeDtypeStruct(a.shape, a.dtype) for a in arrays),
-        in_specs=[vmem] * len(arrays),
-        out_specs=(vmem,) * len(arrays),
+        in_specs=[hbm] * count,
+        out_specs=(hbm,) * count,
+        scratch_shapes=[
+            *[pltpu.VMEM(a.shape, a.dtype) for a in arrays],
+            pltpu.SemaphoreType.DMA((2, count)),
+        ],
         name="copied",
     )(*arrays)
 

time: 145 us -> 142 us (0.979)
  Pallas kernels: 142 us -> 140 us
    pallas_call x1, Pallas kernels: 140 us -> 138 us  [top_network(): pl.pallas_call(top_kernel, out_shape=(jax.ShapeDtypeStruct((4 * rows, col...]
where the time goes in v5:
time: 142 us
  Pallas kernels  140 us (99%)
    pallas_call x1, Pallas kernels, top_network(): pl.pallas_call(top_kernel, out_shape=(jax.ShapeDtypeStruct((4 * rows, col...  138 us

profile of v5, /device:TPU:0, one launch (start us, length us, event | category | flops | bytes accessed | tf_op | source)
XLA Modules:
  0.0 142.1 jit_solution(16590707018493419390)
XLA Ops:
  0.6 1.3 broadcast_in_dim.14.w_out_ref
  1.9 137.6 %top_network.1 = (bf16[512,1024]{1,0:T(8,128)(2,1)}, f32[1,512]{1,0:T(1,128)}, bf16[2048,128]{1,0:T(8,128)(2,1)}) custom-call(s32[16,16384]{1,0:T(8,128)} %bitcast.10, s32[1,16384]{1,0:T(1,128)} %lengths_hbm.1, bf16[2048,128]{1,0:T(8,128)(2,1)} %bitcast.11, bf16[4096,1024]{1,0:T(8,128)(2,1)} %w_first_hbm.1, f32[1,1024]{1,0:T(1,128)} %bitcast.14, ...), custom_call_target="tpu_custom_call" | custom-call | flops 8589934592 | bytes 16777216 | tf_op jit(solution)/shard_map/top_network/pallas_call | solution.py:489
  139.5 2.4 %copied.1 = (bf16[512,1024]{1,0:T(8,128)(2,1)}, f32[1,512]{1,0:T(1,128)}, bf16[2048,128]{1,0:T(8,128)(2,1)}) custom-call(bf16[512,1024]{1,0:T(8,128)(2,1)} %get-tuple-element.9.refs_0_, f32[1,512]{1,0:T(1,128)} %get-tuple-element.10.refs_1_, bf16[2048,128]{1,0:T(8,128)(2,1)} %get-tuple-element.11.refs_2_), custom_call_target="tpu_custom_call" | custom-call | tf_op jit(solution)/shard_map/copied/pallas_call | solution.py:572

commit v6 on v5

--- a/solution.py
+++ b/solution.py
@@ -380,6 +380,7 @@
     def join(chunk):
         middle, begin = 2 * COUNTS[chunk], 4 * starts[chunk]
         parts = (right_part, left_part)
+        onward = near_sums(chunk)
         for k, copy in enumerate(far_copies(chunk)):
             copy.wait_recv()
             summed = k * middle
@@ -387,8 +388,7 @@
             near_out[k, pl.ds(begin + summed, middle), :] = (
                 parts[k][pl.ds(summed, middle), :] + came
             ).astype(jnp.bfloat16)
-        for copy in near_sums(chunk):
-            copy.start()
+            onward[k].start()
 
     def finish(chunk):
         for copy in lone_sums(chunk) + near_sums(chunk):

time: 142 us -> 142 us (level)
  no operation moved by 1% of the time
where the time goes in v6:
time: 142 us
  Pallas kernels  140 us (99%)
    pallas_call x1, Pallas kernels, top_network(): pl.pallas_call(top_kernel, out_shape=(jax.ShapeDtypeStruct((4 * rows, col...  138 us

profile of v6, /device:TPU:0, one launch (start us, length us, event | category | flops | bytes accessed | tf_op | source)
XLA Modules:
  0.0 142.1 jit_solution(8473894971830624917)
XLA Ops:
  0.6 1.3 broadcast_in_dim.14.w_out_ref
  1.9 137.6 %top_network.1 = (bf16[512,1024]{1,0:T(8,128)(2,1)}, f32[1,512]{1,0:T(1,128)}, bf16[2048,128]{1,0:T(8,128)(2,1)}) custom-call(s32[16,16384]{1,0:T(8,128)} %bitcast.10, s32[1,16384]{1,0:T(1,128)} %lengths_hbm.1, bf16[2048,128]{1,0:T(8,128)(2,1)} %bitcast.11, bf16[4096,1024]{1,0:T(8,128)(2,1)} %w_first_hbm.1, f32[1,1024]{1,0:T(1,128)} %bitcast.14, ...), custom_call_target="tpu_custom_call" | custom-call | flops 8589934592 | bytes 16777216 | tf_op jit(solution)/shard_map/top_network/pallas_call | solution.py:489
  139.5 2.4 %copied.1 = (bf16[512,1024]{1,0:T(8,128)(2,1)}, f32[1,512]{1,0:T(1,128)}, bf16[2048,128]{1,0:T(8,128)(2,1)}) custom-call(bf16[512,1024]{1,0:T(8,128)(2,1)} %get-tuple-element.9.refs_0_, f32[1,512]{1,0:T(1,128)} %get-tuple-element.10.refs_1_, bf16[2048,128]{1,0:T(8,128)(2,1)} %get-tuple-element.11.refs_2_), custom_call_target="tpu_custom_call" | custom-call | tf_op jit(solution)/shard_map/copied/pallas_call | solution.py:572
